TPU v7x, 256 devices: a whole 4x4x8 slice. The times are simulated.
256 devices in a mesh: space: 16 (over z_hi, y), src: 16 (over x, z_lo, core).
Axes of the slice: x: 4, y: 4, z: 8 (z_hi: 4, z_lo: 2; z = z_hi * 2 + z_lo), core: 2. Of those that a mesh axis runs over, the one named last changes fastest.
Arguments:
- fields: float32 [6, 125, 16, 16, 256], P(None, None, 'src', 'space'), may hold values from -6 to 6
- cotangent: float32 [6, 125, 16, 16, 256], P(None, None, 'src', 'space'), may hold values from -1.5 to 1.5
- permittivity: float32 [16, 256], P('space'), may hold values from 1 to 4
- regions: int32 [16, 256], P('space'), may hold values from 0 to 7
- conductance: float32 [8], replicated, may hold values from 2 to 20
- src_layer: int32 [16], P('src'), may hold values from 0 to 15
- src_cell: int32 [16], P('src'), may hold values from 0 to 255
- src_node: int32 [16], P('src'), may hold values from 0 to 124
- src_amp: float32 [16, 6], P('src'), may hold values from -600 to 600
Outputs:
- adjoint: float32 [6, 125, 16, 16, 256], P(None, None, 'src', 'space')
- gradient: float32 [16, 256], P('space')
All inputs are finite; a program needn't handle non-finite values.
Results may differ from a plain program's by a relative error of at most 0.0003.
Values sent between devices are 32-bit elements; how exact they have to be, the bound alone decides.
No kernel may reach another device: no remote copies, remote signals or barrier semaphores. Data moves between devices by JAX's collectives and lax.ppermute only.
A program may use at most 128 MiB of HBM per device.

v0:
```python
import math

import jax
import jax.numpy as jnp
import numpy as np
from jax import lax
from jax.sharding import PartitionSpec as P

EZ = 16


TIME_STEP = 0.02
PENALTY = 1.0
LIFT_SCALE = 20.0
METRIC = 2.0


def padded(x, sides, width):
    for axis, dim in sides:
        peers, length = (lax.axis_size(axis), x.shape[dim])
        up = [(i, (i + 1) % peers) for i in range(peers - 1)]
        down = [(j, i) for i, j in up]
        last = lax.slice_in_dim(x, length - width, length, axis=dim)
        initial = lax.slice_in_dim(x, 0, width, axis=dim)
        before = lax.ppermute(last, axis, up)
        after = lax.ppermute(initial, axis, down)
        x = jnp.concatenate([before, x, after], axis=dim)
    return x


def gll_derivative():
    points = np.array([-1.0, -math.sqrt(3.0 / 7.0), 0.0, math.sqrt(3.0 / 7.0), 1.0])
    products = np.array(
        [
            np.prod(
                [
                    points[row_index] - points[column_index]
                    for column_index in range(5)
                    if column_index != row_index
                ]
            )
            for row_index in range(5)
        ]
    )
    matrix = np.zeros((5, 5))
    for row_index in range(5):
        for column_index in range(5):
            if column_index != row_index:
                matrix[row_index, column_index] = products[row_index] / (
                    products[column_index] * (points[row_index] - points[column_index])
                )
    for row_index in range(5):
        matrix[row_index, row_index] = -np.sum(matrix[row_index])
    return matrix


def derive(values, direction):
    matrix = jnp.asarray(gll_derivative() * METRIC, dtype=jnp.float32)
    patterns = ("ij,cj...->ci...", "ij,caj...->cai...", "ij,cabj...->cabi...")
    return jnp.einsum(patterns[direction], matrix, values, precision=lax.Precision.HIGHEST)


def curl(values):
    first_slope = derive(values, 0)
    second_slope = derive(values, 1)
    third_slope = derive(values, 2)
    return jnp.stack(
        [
            second_slope[2] - third_slope[1],
            third_slope[0] - first_slope[2],
            first_slope[1] - second_slope[0],
        ]
    )


def face_slice(values, normal_axis, face_side):
    face_node = 0 if face_side == 0 else 4
    if normal_axis == 0:
        return values[:, face_node]
    if normal_axis == 1:
        return values[:, :, face_node]
    return values[:, :, :, face_node]


def face_add(values, normal_axis, face_side, addend):
    face_node = 0 if face_side == 0 else 4
    if normal_axis == 0:
        return values.at[:, face_node].add(addend)
    if normal_axis == 1:
        return values.at[:, :, face_node].add(addend)
    return values.at[:, :, :, face_node].add(addend)


def outside(values, outer, normal_axis, face_side):
    if normal_axis == 0:
        if face_side == 0:
            return jnp.concatenate(
                [outer[..., :1, :], face_slice(values, 0, 1)[..., :-1, :]], axis=-2
            )
        return jnp.concatenate([face_slice(values, 0, 0)[..., 1:, :], outer[..., 1:, :]], axis=-2)
    facing = face_slice(values, normal_axis, 1 - face_side)
    if normal_axis == 1:
        return jnp.roll(facing, EZ if face_side == 0 else -EZ, axis=-1)
    column = jnp.arange(facing.shape[-1], dtype=jnp.int32) % EZ
    if face_side == 0:
        return jnp.where(
            column == 0, jnp.roll(facing, 1 - EZ, axis=-1), jnp.roll(facing, 1, axis=-1)
        )
    return jnp.where(
        column == EZ - 1, jnp.roll(facing, EZ - 1, axis=-1), jnp.roll(facing, -1, axis=-1)
    )


def normal_cross(normal_axis, normal_sign, vector):
    empty = jnp.zeros_like(vector[0])
    if normal_axis == 0:
        pieces = [empty, -vector[2], vector[1]]
    elif normal_axis == 1:
        pieces = [vector[2], empty, -vector[0]]
    else:
        pieces = [-vector[1], vector[0], empty]
    return normal_sign * jnp.stack(pieces)


def double_cross(normal_axis, vector):
    pieces = [
        jnp.zeros_like(vector[0]) if component == normal_axis else -vector[component]
        for component in range(3)
    ]
    return jnp.stack(pieces)


def rhs_field(curled, penalised, outer_curled, outer_penalised, orient):
    result = orient * curl(curled)
    for normal_axis in range(3):
        for face_side in range(2):
            normal_sign = -1.0 if face_side == 0 else 1.0
            jump_curled = face_slice(curled, normal_axis, face_side) - outside(
                curled, outer_curled, normal_axis, face_side
            )
            jump_penalised = face_slice(penalised, normal_axis, face_side) - outside(
                penalised, outer_penalised, normal_axis, face_side
            )
            face_flux = -0.5 * orient * normal_cross(
                normal_axis, normal_sign, jump_curled
            ) + 0.5 * PENALTY * double_cross(normal_axis, jump_penalised)
            result = face_add(result, normal_axis, face_side, LIFT_SCALE * face_flux)
    return result


def conductivity(regions, conductance):
    matches = regions[..., None] == jnp.arange(conductance.shape[0], dtype=jnp.int32)
    return jnp.sum(jnp.where(matches, conductance, 0.0), axis=-1)


def source_terms(layer_index, cell_index, node_index, amplitude, layers, cell_count):
    layer_match = (layer_index[:, None] == jnp.arange(layers, dtype=jnp.int32)[None, :]).astype(
        jnp.float32
    )
    cell_match = (cell_index[:, None] == jnp.arange(cell_count, dtype=jnp.int32)[None, :]).astype(
        jnp.float32
    )
    node_match = (node_index[:, None] == jnp.arange(125, dtype=jnp.int32)[None, :]).astype(
        jnp.float32
    )
    placed = (
        node_match.T[:, :, None, None] * (layer_match[:, :, None] * cell_match[:, None, :])[None]
    )
    source_list = []
    for time_index in range(amplitude.shape[1] // 3):
        weights = amplitude[:, 3 * time_index : 3 * time_index + 3].T
        source_term = weights[:, None, :, None, None] * placed[None]
        source_list.append(source_term.reshape((3, 5, 5, 5) + placed.shape[1:]))
    return source_list


def boundary(values):
    return jnp.concatenate([face_slice(values, 0, 0), face_slice(values, 0, 1)], axis=-2)


def outer_pair(haloed):
    return jnp.concatenate([haloed[..., :1, :], haloed[..., -1:, :]], axis=-2)


def deposit(values, returned):
    values = values.at[:, 0, :, :, :, 0, :].add(returned[:, :, :, :, 0, :])
    return values.at[:, 4, :, :, :, -1, :].add(returned[:, :, :, :, 1, :])


def primal_traces(outgoing):
    return outer_pair(padded(outgoing, (("space", 4),), 1))


def returned_traces(outgoing):
    return outer_pair(padded(outgoing, (("space", 4),), 1))


def trace_anchor(values):
    return jnp.zeros(values.shape[:3] + (values.shape[4], 2, values.shape[6]), jnp.float32)


def electric_transpose(dual_electric, dual_magnetic, coefficient, damping):
    weighted = coefficient * dual_electric

    def electric_operator(magnetic, electric, outer_magnetic, outer_electric):
        return rhs_field(magnetic, electric, outer_magnetic, outer_electric, 1.0)

    field_anchor = jnp.zeros_like(dual_electric)
    outer_anchor = trace_anchor(dual_electric)
    unused, pullback = jax.vjp(
        electric_operator, field_anchor, field_anchor, outer_anchor, outer_anchor
    )
    back_magnetic, back_electric, return_magnetic, return_electric = pullback(weighted)
    return (
        dual_electric + back_electric - damping * weighted,
        dual_magnetic + back_magnetic,
        return_magnetic,
        return_electric,
    )


def magnetic_transpose(dual_electric, dual_magnetic):
    weighted = TIME_STEP * dual_magnetic

    def magnetic_operator(electric, magnetic, outer_electric, outer_magnetic):
        return rhs_field(electric, magnetic, outer_electric, outer_magnetic, -1.0)

    field_anchor = jnp.zeros_like(dual_electric)
    outer_anchor = trace_anchor(dual_electric)
    unused, pullback = jax.vjp(
        magnetic_operator, field_anchor, field_anchor, outer_anchor, outer_anchor
    )
    back_electric, back_magnetic, return_electric, return_magnetic = pullback(weighted)
    return (
        dual_electric + back_electric,
        dual_magnetic + back_magnetic,
        return_electric,
        return_magnetic,
    )


def on_device(
    fields, cotangent, permittivity, regions, conductance, src_layer, src_cell, src_node, src_amp
):
    layers = fields.shape[3]
    cell_count = fields.shape[4]
    nodal_shape = (6, 5, 5, 5) + fields.shape[2:]
    fields_now = fields.reshape(nodal_shape)
    dual_fields = cotangent.reshape(nodal_shape)
    electric, magnetic = (fields_now[:3], fields_now[3:])
    dual_electric, dual_magnetic = (dual_fields[:3], dual_fields[3:])
    coefficient = TIME_STEP / permittivity
    damping = conductivity(regions, conductance)
    first_layer = lax.axis_index("space") * layers
    source_list = source_terms(
        src_layer - first_layer, src_cell, src_node, src_amp, layers, cell_count
    )
    steps_total = len(source_list)
    forcings = [None] * steps_total
    incoming = [None] * steps_total
    for time_index in range(steps_total):
        received = primal_traces(jnp.concatenate([boundary(electric), boundary(magnetic)], axis=0))
        magnetic_next = magnetic + TIME_STEP * rhs_field(
            electric, magnetic, received[:3], received[3:], -1.0
        )
        received_next = primal_traces(boundary(magnetic_next))
        forcing = (
            rhs_field(magnetic_next, electric, received_next, received[:3], 1.0)
            - damping * electric
            + source_list[time_index]
        )
        forcings[time_index] = forcing
        if time_index + 1 < steps_total:
            electric = electric + coefficient * forcing
        magnetic = magnetic_next
    for time_index in reversed(range(steps_total)):
        incoming[time_index] = dual_electric
        dual_electric, dual_magnetic, return_magnetic, return_electric = electric_transpose(
            dual_electric, dual_magnetic, coefficient, damping
        )
        dual_magnetic = deposit(dual_magnetic, returned_traces(return_magnetic))
        dual_electric, dual_magnetic, extra_electric, extra_magnetic = magnetic_transpose(
            dual_electric, dual_magnetic
        )
        sent_back = returned_traces(
            jnp.concatenate([return_electric + extra_electric, extra_magnetic], axis=0)
        )
        dual_electric = deposit(dual_electric, sent_back[:3])
        dual_magnetic = deposit(dual_magnetic, sent_back[3:])
    partial_sum = jnp.zeros_like(permittivity)
    for time_index in range(steps_total):
        partial_sum = partial_sum + jnp.sum(
            incoming[time_index] * forcings[time_index], axis=(0, 1, 2, 3, 4)
        )
    local_gradient = -TIME_STEP / (permittivity * permittivity) * partial_sum
    gradient = lax.psum(local_gradient, "src")
    adjoint = jnp.concatenate([dual_electric, dual_magnetic], axis=0).reshape(fields.shape)
    return (adjoint, gradient)


def solution(mesh):
    return jax.shard_map(
        on_device,
        mesh=mesh,
        in_specs=(
            P(None, None, "src", "space", None),
            P(None, None, "src", "space", None),
            P("space", None),
            P("space", None),
            P(),
            P("src"),
            P("src"),
            P("src"),
            P("src", None),
        ),
        out_specs=(P(None, None, "src", "space", None), P("space", None)),
        check_vma=False,
    )
```

profile of v0, /device:TPU:89, one launch (start us, length us, event | category | flops | bytes accessed | tf_op | source)
XLA Modules:
  0.0 324.2 jit_solution(18265742573547592756)
XLA Ops:
  0.6 2.4 fusion.456
  6.0 5.8 %collective-permute-start = (f32[3,5,5,1,1,256]{5,2,1,4,3,0:T(8,128)}, f32[3,5,5,1,1,256]{5,2,1,4,3,0:T(8,128)}, u32[]{:S(2)}, u32[]{:S(2)}) collective-permute-start(f32[3,5,5,1,1,256]{5,2,1,4,3,0:T(8,128)} %get-tuple-element.614), channel_id=1, source_target_pairs={{0,16},{16,32},{32,48},{48,64},{64,80},{80,96},{96,112},{112,128},... | collective-permute-start | bytes 230408 | tf_op jit(solution)/shard_map/ppermute | solution.py:25
  11.8 1.9 collective-permute-start.1
  17.1 1.9 collective-permute-start.9
  19.0 7.8 %collective-permute-start.8 = (f32[6,5,5,1,1,256]{5,2,1,4,3,0:T(8,128)}, f32[6,5,5,1,1,256]{5,2,1,4,3,0:T(8,128)}, u32[]{:S(2)}, u32[]{:S(2)}) collective-permute-start(f32[6,5,5,1,1,256]{5,2,1,4,3,0:T(8,128)} %get-tuple-element.578), channel_id=1, source_target_pairs={{0,16},{16,32},{32,48},{48,64},{64,80},{80,96},{96,112},{112,128},... | collective-permute-start | bytes 460808 | tf_op jit(solution)/shard_map/ppermute | solution.py:25
  54.7 1.6 fusion.74
  81.0 1.7 fusion.23
  87.9 1.7 fusion.291
  103.4 3.3 %collective-permute-start.2 = (f32[6,5,5,1,1,256]{5,2,0,1,4,3:T(8,128)}, f32[6,5,5,1,1,256]{5,2,0,1,4,3:T(8,128)}, u32[]{:S(2)}, u32[]{:S(2)}) collective-permute-start(f32[6,5,5,1,1,256]{5,2,0,1,4,3:T(8,128)} %get-tuple-element.582), channel_id=1, source_target_pairs={{0,16},{16,32},{32,48},{48,64},{64,80},{80,96},{96,112},{112,128},... | collective-permute-start | bytes 460808 | tf_op jit(solution)/shard_map/ppermute | solution.py:25
  106.8 1.9 collective-permute-start.3
  119.3 2.6 scatter-add.146
  123.2 2.6 scatter-add.149
  136.0 1.9 collective-permute-start.11
  138.0 7.7 %collective-permute-start.10 = (f32[3,5,5,1,1,256]{5,2,1,4,3,0:T(8,128)S(1)}, f32[3,5,5,1,1,256]{5,2,1,4,3,0:T(8,128)S(1)}, u32[]{:S(2)}, u32[]{:S(2)}) collective-permute-start(f32[3,5,5,1,1,256]{5,2,1,4,3,0:T(8,128)S(1)} %get-tuple-element.506), channel_id=1, source_target_pairs={{0,16},{16,32},{32,48},{48,64},{64,80},{80,96},{96,112},{112,128},... | collective-permute-start | bytes 230408 | tf_op jit(solution)/shard_map/ppermute | solution.py:25
  150.6 1.9 fusion.230
  170.5 2.7 scatter-add.156
  174.5 2.7 scatter-add.159
  187.4 3.4 %collective-permute-start.4 = (f32[3,5,5,1,1,256]{5,2,1,4,3,0:T(8,128)S(1)}, f32[3,5,5,1,1,256]{5,2,1,4,3,0:T(8,128)S(1)}, u32[]{:S(2)}, u32[]{:S(2)}) collective-permute-start(f32[3,5,5,1,1,256]{5,2,1,4,3,0:T(8,128)S(1)} %get-tuple-element.608), channel_id=1, source_target_pairs={{0,16},{16,32},{32,48},{48,64},{64,80},{80,96},{96,112},{112,128},... | collective-permute-start | bytes 230408 | tf_op jit(solution)/shard_map/ppermute | solution.py:25
  190.8 2.1 collective-permute-start.5
  194.7 2.1 collective-permute-start.13
  196.8 7.6 %collective-permute-start.12 = (f32[6,5,5,1,1,256]{5,2,1,4,3,0:T(8,128)S(1)}, f32[6,5,5,1,1,256]{5,2,1,4,3,0:T(8,128)S(1)}, u32[]{:S(2)}, u32[]{:S(2)}) collective-permute-start(f32[6,5,5,1,1,256]{5,2,1,4,3,0:T(8,128)S(1)} %get-tuple-element.576), channel_id=1, source_target_pairs={{0,16},{16,32},{32,48},{48,64},{64,80},{80,96},{96,112},{112,128},... | collective-permute-start | bytes 460808 | tf_op jit(solution)/shard_map/ppermute | solution.py:25
  226.7 3.3 %collective-permute-start.6 = (f32[6,5,5,1,1,256]{5,2,1,0,4,3:T(8,128)}, f32[6,5,5,1,1,256]{5,2,1,0,4,3:T(8,128)}, u32[]{:S(2)}, u32[]{:S(2)}) collective-permute-start(f32[6,5,5,1,1,256]{5,2,1,0,4,3:T(8,128)} %get-tuple-element.580), channel_id=1, source_target_pairs={{0,16},{16,32},{32,48},{48,64},{64,80},{80,96},{96,112},{112,128},... | collective-permute-start | bytes 460808 | tf_op jit(solution)/shard_map/ppermute | solution.py:25
  230.1 2.2 collective-permute-start.7
  245.1 2.6 scatter-add.166
  249.0 2.6 scatter-add.169
  264.4 1.9 collective-permute-start.15
  266.3 7.9 %collective-permute-start.14 = (f32[3,5,5,1,1,256]{5,2,1,4,3,0:T(8,128)}, f32[3,5,5,1,1,256]{5,2,1,4,3,0:T(8,128)}, u32[]{:S(2)}, u32[]{:S(2)}) collective-permute-start(f32[3,5,5,1,1,256]{5,2,1,4,3,0:T(8,128)} %get-tuple-element.476), channel_id=1, source_target_pairs={{0,16},{16,32},{32,48},{48,64},{64,80},{80,96},{96,112},{112,128},... | collective-permute-start | bytes 230408 | tf_op jit(solution)/shard_map/ppermute | solution.py:25
  275.7 1.6 fusion.14
  280.5 1.7 reshape.6541
  284.9 3.1 scatter-add.176
  288.3 3.1 scatter-add.179
  291.8 31.9 %psum.7 = f32[1,256]{1,0:T(1,128)} all-reduce(f32[1,256]{1,0:T(1,128)S(1)} %divide_multiply_fusion), channel_id=1, replica_groups=mesh['space'=16,'src'=16] {'src'}, use_global_device_ids=true, to_apply=%region_3.4 | all-reduce | flops 256 | bytes 2048 | tf_op jit(solution)/shard_map/psum | solution.py:296
  (1014 shorter events, 186.6 us)
Async XLA Ops:
  6.0 78.5 %collective-permute-start = (f32[3,5,5,1,1,256]{5,2,1,4,3,0:T(8,128)}, f32[3,5,5,1,1,256]{5,2,1,4,3,0:T(8,128)}, u32[]{:S(2)}, u32[]{:S(2)}) collective-permute-start(f32[3,5,5,1,1,256]{5,2,1,4,3,0:T(8,128)} %get-tuple-element.614), channel_id=1, source_target_pairs={{0,16},{16,32},{32,48},{48,64},{64,80},{80,96},{96,112},{112,128},... | collective-permute-start | bytes 230408 | tf_op jit(solution)/shard_map/ppermute | solution.py:25
  11.8 73.7 %collective-permute-start.1 = (f32[3,5,5,1,1,256]{5,2,1,4,3,0:T(8,128)}, f32[3,5,5,1,1,256]{5,2,1,4,3,0:T(8,128)}, u32[]{:S(2)}, u32[]{:S(2)}) collective-permute-start(f32[3,5,5,1,1,256]{5,2,1,4,3,0:T(8,128)} %get-tuple-element.613), channel_id=1, source_target_pairs={{16,0},{32,16},{48,32},{64,48},{80,64},{96,80},{112,96},{128,112},... | collective-permute-start | bytes 230408 | tf_op jit(solution)/shard_map/ppermute | solution.py:26
  15.2 33.0 %copy-start.2 = (f32[3,125,1,1,256]{4,3,2,1,0:T(1,128)}, f32[3,125,1,1,256]{4,3,2,1,0:T(1,128)S(1)}, u32[]{:S(2)}) copy-start(f32[3,125,1,1,256]{4,3,2,1,0:T(1,128)S(1)} %get-tuple-element.466) | copy-start | bytes 1152004
  15.2 76.1 %copy-start = (f32[3,125,1,1,256]{4,3,2,1,0:T(1,128)}, f32[3,125,1,1,256]{4,3,2,1,0:T(1,128)S(1)}, u32[]{:S(2)}) copy-start(f32[3,125,1,1,256]{4,3,2,1,0:T(1,128)S(1)} %get-tuple-element.465) | copy-start | bytes 1152004
  17.1 95.0 %collective-permute-start.9 = (f32[6,5,5,1,1,256]{5,2,1,4,3,0:T(8,128)}, f32[6,5,5,1,1,256]{5,2,1,4,3,0:T(8,128)}, u32[]{:S(2)}, u32[]{:S(2)}) collective-permute-start(f32[6,5,5,1,1,256]{5,2,1,4,3,0:T(8,128)} %get-tuple-element.577), channel_id=1, source_target_pairs={{16,0},{32,16},{48,32},{64,48},{80,64},{96,80},{112,96},{128,112},... | collective-permute-start | bytes 460808 | tf_op jit(solution)/shard_map/ppermute | solution.py:26
  19.0 93.1 %collective-permute-start.8 = (f32[6,5,5,1,1,256]{5,2,1,4,3,0:T(8,128)}, f32[6,5,5,1,1,256]{5,2,1,4,3,0:T(8,128)}, u32[]{:S(2)}, u32[]{:S(2)}) collective-permute-start(f32[6,5,5,1,1,256]{5,2,1,4,3,0:T(8,128)} %get-tuple-element.578), channel_id=1, source_target_pairs={{0,16},{16,32},{32,48},{48,64},{64,80},{80,96},{96,112},{112,128},... | collective-permute-start | bytes 460808 | tf_op jit(solution)/shard_map/ppermute | solution.py:25
  30.6 60.8 %copy-start.231 = (pred[256]{0:T(512)(128)(4,1)}, pred[256]{0:T(512)(128)(4,1)S(1)}, u32[]{:S(2)}) copy-start(pred[256]{0:T(512)(128)(4,1)S(1)} %get-tuple-element.923) | copy-start | bytes 772
  103.4 46.1 %collective-permute-start.2 = (f32[6,5,5,1,1,256]{5,2,0,1,4,3:T(8,128)}, f32[6,5,5,1,1,256]{5,2,0,1,4,3:T(8,128)}, u32[]{:S(2)}, u32[]{:S(2)}) collective-permute-start(f32[6,5,5,1,1,256]{5,2,0,1,4,3:T(8,128)} %get-tuple-element.582), channel_id=1, source_target_pairs={{0,16},{16,32},{32,48},{48,64},{64,80},{80,96},{96,112},{112,128},... | collective-permute-start | bytes 460808 | tf_op jit(solution)/shard_map/ppermute | solution.py:25
  106.8 43.8 %collective-permute-start.3 = (f32[6,5,5,1,1,256]{5,2,0,1,4,3:T(8,128)}, f32[6,5,5,1,1,256]{5,2,0,1,4,3:T(8,128)}, u32[]{:S(2)}, u32[]{:S(2)}) collective-permute-start(f32[6,5,5,1,1,256]{5,2,0,1,4,3:T(8,128)} %get-tuple-element.581), channel_id=1, source_target_pairs={{16,0},{32,16},{48,32},{64,48},{80,64},{96,80},{112,96},{128,112},... | collective-permute-start | bytes 460808 | tf_op jit(solution)/shard_map/ppermute | solution.py:26
  136.0 30.0 %collective-permute-start.11 = (f32[3,5,5,1,1,256]{5,2,1,4,3,0:T(8,128)S(1)}, f32[3,5,5,1,1,256]{5,2,1,4,3,0:T(8,128)S(1)}, u32[]{:S(2)}, u32[]{:S(2)}) collective-permute-start(f32[3,5,5,1,1,256]{5,2,1,4,3,0:T(8,128)S(1)} %get-tuple-element.505), channel_id=1, source_target_pairs={{16,0},{32,16},{48,32},{64,48},{80,64},{96,80},{112,96},{128,112},... | collective-permute-start | bytes 230408 | tf_op jit(solution)/shard_map/ppermute | solution.py:26
  138.0 28.0 %collective-permute-start.10 = (f32[3,5,5,1,1,256]{5,2,1,4,3,0:T(8,128)S(1)}, f32[3,5,5,1,1,256]{5,2,1,4,3,0:T(8,128)S(1)}, u32[]{:S(2)}, u32[]{:S(2)}) collective-permute-start(f32[3,5,5,1,1,256]{5,2,1,4,3,0:T(8,128)S(1)} %get-tuple-element.506), channel_id=1, source_target_pairs={{0,16},{16,32},{32,48},{48,64},{64,80},{80,96},{96,112},{112,128},... | collective-permute-start | bytes 230408 | tf_op jit(solution)/shard_map/ppermute | solution.py:25
  146.7 21.9 %copy-start.103 = (f32[1,5,1,5,1,1,256]{6,3,1,5,4,2,0:T(8,128)}, f32[1,5,1,5,1,1,256]{6,3,1,5,4,2,0:T(8,128)S(1)}, u32[]{:S(2)}) copy-start(f32[1,5,1,5,1,1,256]{6,3,1,5,4,2,0:T(8,128)S(1)} %fusion.331) | copy-start | bytes 76804
  149.5 17.4 %copy-start.117 = (f32[1,5,1,5,1,1,256]{6,3,1,5,4,2,0:T(8,128)}, f32[1,5,1,5,1,1,256]{6,3,1,5,4,2,0:T(8,128)S(1)}, u32[]{:S(2)}) copy-start(f32[1,5,1,5,1,1,256]{6,3,1,5,4,2,0:T(8,128)S(1)} %fusion.332) | copy-start | bytes 76804
  187.4 27.2 %collective-permute-start.4 = (f32[3,5,5,1,1,256]{5,2,1,4,3,0:T(8,128)S(1)}, f32[3,5,5,1,1,256]{5,2,1,4,3,0:T(8,128)S(1)}, u32[]{:S(2)}, u32[]{:S(2)}) collective-permute-start(f32[3,5,5,1,1,256]{5,2,1,4,3,0:T(8,128)S(1)} %get-tuple-element.608), channel_id=1, source_target_pairs={{0,16},{16,32},{32,48},{48,64},{64,80},{80,96},{96,112},{112,128},... | collective-permute-start | bytes 230408 | tf_op jit(solution)/shard_map/ppermute | solution.py:25
  190.8 23.8 %collective-permute-start.5 = (f32[3,5,5,1,1,256]{5,2,1,4,3,0:T(8,128)S(1)}, f32[3,5,5,1,1,256]{5,2,1,4,3,0:T(8,128)S(1)}, u32[]{:S(2)}, u32[]{:S(2)}) collective-permute-start(f32[3,5,5,1,1,256]{5,2,1,4,3,0:T(8,128)S(1)} %get-tuple-element.607), channel_id=1, source_target_pairs={{16,0},{32,16},{48,32},{64,48},{80,64},{96,80},{112,96},{128,112},... | collective-permute-start | bytes 230408 | tf_op jit(solution)/shard_map/ppermute | solution.py:26
  194.6 12.7 %copy-start.130 = (f32[3,5,5,1,1,1,256]{6,4,2,1,0,5,3:T(1,128)S(1)}, f32[3,5,5,1,1,1,256]{6,4,2,1,0,5,3:T(1,128)}, u32[]{:S(2)}) copy-start(f32[3,5,5,1,1,1,256]{6,4,2,1,0,5,3:T(1,128)} %get-tuple-element.863) | copy-start | bytes 230404
  194.6 13.4 %copy-start.95 = (f32[3,5,5,1,1,256]{5,3,4,2,1,0:T(1,128)S(1)}, f32[3,5,5,1,1,256]{5,3,4,2,1,0:T(1,128)}, u32[]{:S(2)}) copy-start(f32[3,5,5,1,1,256]{5,3,4,2,1,0:T(1,128)} %get-tuple-element.833) | copy-start | bytes 230404
  194.6 14.7 %copy-start.174 = (f32[3,5,5,1,1,1,256]{6,3,5,4,2,1,0:T(1,128)S(1)}, f32[3,5,5,1,1,1,256]{6,3,5,4,2,1,0:T(1,128)}, u32[]{:S(2)}) copy-start(f32[3,5,5,1,1,1,256]{6,3,5,4,2,1,0:T(1,128)} %get-tuple-element.806) | copy-start | bytes 230404
  194.7 44.0 %collective-permute-start.13 = (f32[6,5,5,1,1,256]{5,2,1,4,3,0:T(8,128)S(1)}, f32[6,5,5,1,1,256]{5,2,1,4,3,0:T(8,128)S(1)}, u32[]{:S(2)}, u32[]{:S(2)}) collective-permute-start(f32[6,5,5,1,1,256]{5,2,1,4,3,0:T(8,128)S(1)} %get-tuple-element.575), channel_id=1, source_target_pairs={{16,0},{32,16},{48,32},{64,48},{80,64},{96,80},{112,96},{128,112},... | collective-permute-start | bytes 460808 | tf_op jit(solution)/shard_map/ppermute | solution.py:26
  196.8 41.9 %collective-permute-start.12 = (f32[6,5,5,1,1,256]{5,2,1,4,3,0:T(8,128)S(1)}, f32[6,5,5,1,1,256]{5,2,1,4,3,0:T(8,128)S(1)}, u32[]{:S(2)}, u32[]{:S(2)}) collective-permute-start(f32[6,5,5,1,1,256]{5,2,1,4,3,0:T(8,128)S(1)} %get-tuple-element.576), channel_id=1, source_target_pairs={{0,16},{16,32},{32,48},{48,64},{64,80},{80,96},{96,112},{112,128},... | collective-permute-start | bytes 460808 | tf_op jit(solution)/shard_map/ppermute | solution.py:25
  221.6 22.2 %copy-start.172 = (f32[1,5,5,1,1,1,256]{6,3,5,4,2,1,0:T(1,128)}, f32[1,5,5,1,1,1,256]{6,3,5,4,2,1,0:T(1,128)S(1)}, u32[]{:S(2)}) copy-start(f32[1,5,5,1,1,1,256]{6,3,5,4,2,1,0:T(1,128)S(1)} %get-tuple-element.783) | copy-start | bytes 76804
  226.7 50.8 %collective-permute-start.6 = (f32[6,5,5,1,1,256]{5,2,1,0,4,3:T(8,128)}, f32[6,5,5,1,1,256]{5,2,1,0,4,3:T(8,128)}, u32[]{:S(2)}, u32[]{:S(2)}) collective-permute-start(f32[6,5,5,1,1,256]{5,2,1,0,4,3:T(8,128)} %get-tuple-element.580), channel_id=1, source_target_pairs={{0,16},{16,32},{32,48},{48,64},{64,80},{80,96},{96,112},{112,128},... | collective-permute-start | bytes 460808 | tf_op jit(solution)/shard_map/ppermute | solution.py:25
  230.1 49.3 %collective-permute-start.7 = (f32[6,5,5,1,1,256]{5,2,1,0,4,3:T(8,128)}, f32[6,5,5,1,1,256]{5,2,1,0,4,3:T(8,128)}, u32[]{:S(2)}, u32[]{:S(2)}) collective-permute-start(f32[6,5,5,1,1,256]{5,2,1,0,4,3:T(8,128)} %get-tuple-element.579), channel_id=1, source_target_pairs={{16,0},{32,16},{48,32},{64,48},{80,64},{96,80},{112,96},{128,112},... | collective-permute-start | bytes 460808 | tf_op jit(solution)/shard_map/ppermute | solution.py:26
  263.1 12.3 %copy-start.52 = (f32[3,5,1,5,1,1,256]{6,3,1,0,5,4,2:T(8,128)S(1)}, f32[3,5,1,5,1,1,256]{6,3,1,0,5,4,2:T(8,128)}, u32[]{:S(2)}) copy-start(f32[3,5,1,5,1,1,256]{6,3,1,0,5,4,2:T(8,128)} %get-tuple-element.733) | copy-start | bytes 230404
  263.2 12.3 %copy-start.53 = (f32[3,1,5,5,1,1,256]{6,3,2,0,5,4,1:T(8,128)S(1)}, f32[3,1,5,5,1,1,256]{6,3,2,0,5,4,1:T(8,128)}, u32[]{:S(2)}) copy-start(f32[3,1,5,5,1,1,256]{6,3,2,0,5,4,1:T(8,128)} %get-tuple-element.726) | copy-start | bytes 230404
  263.2 12.3 %copy-start.58 = (f32[3,5,1,5,1,1,256]{6,3,2,0,5,4,1:T(8,128)S(1)}, f32[3,5,1,5,1,1,256]{6,3,2,0,5,4,1:T(8,128)}, u32[]{:S(2)}) copy-start(f32[3,5,1,5,1,1,256]{6,3,2,0,5,4,1:T(8,128)} %get-tuple-element.720) | copy-start | bytes 230404
  263.2 12.3 %copy-start.59 = (f32[3,1,5,5,1,1,256]{6,3,2,0,5,4,1:T(8,128)S(1)}, f32[3,1,5,5,1,1,256]{6,3,2,0,5,4,1:T(8,128)}, u32[]{:S(2)}) copy-start(f32[3,1,5,5,1,1,256]{6,3,2,0,5,4,1:T(8,128)} %get-tuple-element.724) | copy-start | bytes 230404
  263.2 12.3 %copy-start.60 = (f32[3,5,1,5,1,1,256]{6,3,0,1,5,4,2:T(8,128)S(1)}, f32[3,5,1,5,1,1,256]{6,3,0,1,5,4,2:T(8,128)}, u32[]{:S(2)}) copy-start(f32[3,5,1,5,1,1,256]{6,3,0,1,5,4,2:T(8,128)} %get-tuple-element.731) | copy-start | bytes 230404
  263.2 12.3 %copy-start.61 = (f32[3,1,5,5,1,1,256]{6,3,2,0,5,4,1:T(8,128)S(1)}, f32[3,1,5,5,1,1,256]{6,3,2,0,5,4,1:T(8,128)}, u32[]{:S(2)}) copy-start(f32[3,1,5,5,1,1,256]{6,3,2,0,5,4,1:T(8,128)} %get-tuple-element.722) | copy-start | bytes 230404
  263.2 12.3 %copy-start.62 = (f32[3,5,1,5,1,1,256]{6,3,0,1,5,4,2:T(8,128)S(1)}, f32[3,5,1,5,1,1,256]{6,3,0,1,5,4,2:T(8,128)}, u32[]{:S(2)}) copy-start(f32[3,5,1,5,1,1,256]{6,3,0,1,5,4,2:T(8,128)} %add_bitcast_fusion.19) | copy-start | bytes 230404
  264.4 17.9 %collective-permute-start.15 = (f32[3,5,5,1,1,256]{5,2,1,4,3,0:T(8,128)}, f32[3,5,5,1,1,256]{5,2,1,4,3,0:T(8,128)}, u32[]{:S(2)}, u32[]{:S(2)}) collective-permute-start(f32[3,5,5,1,1,256]{5,2,1,4,3,0:T(8,128)} %get-tuple-element.475), channel_id=1, source_target_pairs={{16,0},{32,16},{48,32},{64,48},{80,64},{96,80},{112,96},{128,112},... | collective-permute-start | bytes 230408 | tf_op jit(solution)/shard_map/ppermute | solution.py:26
  266.3 15.9 %collective-permute-start.14 = (f32[3,5,5,1,1,256]{5,2,1,4,3,0:T(8,128)}, f32[3,5,5,1,1,256]{5,2,1,4,3,0:T(8,128)}, u32[]{:S(2)}, u32[]{:S(2)}) collective-permute-start(f32[3,5,5,1,1,256]{5,2,1,4,3,0:T(8,128)} %get-tuple-element.476), channel_id=1, source_target_pairs={{0,16},{16,32},{32,48},{48,64},{64,80},{80,96},{96,112},{112,128},... | collective-permute-start | bytes 230408 | tf_op jit(solution)/shard_map/ppermute | solution.py:25
  (231 other events, 855.9 us)
where the time goes:
time: 329 us; the launch traced here: 324 us
  other arithmetic  105 us (32%)
  local copies, waits for them, and re-layouts  94.9 us (29%)
  starting transfers between devices  62.8 us (19%)
  blocking collectives  31.9 us (10%)
  matrix products  21.3 us (6%)
  between operations  8.24 us (3%)
    ppermute x8, starting transfers between devices, padded(): before = lax.ppermute(last, axis, up)  46.8 us
    psum x1, blocking collectives, on_device(): gradient = lax.psum(local_gradient, 'src')  31.9 us
    scatter-add x8, local copies, waits for them, and re-layouts, face_add(): return values.at[:, :, :, face_node].add(addend)  22.1 us
    dot_general x24, matrix products, derive(): jnp.einsum(patterns[direction], matrix, values, precision=lax.Precision.H...  21.3 us
    ppermute x8, starting transfers between devices, padded(): after = lax.ppermute(initial, axis, down)  16 us
    broadcast_in_dim x28, local copies, waits for them, and re-layouts, face_slice(): return values[:, :, :, face_node]  13.6 us
    another operation x25, other arithmetic, double_cross(): return jnp.stack(pieces)  11.2 us
    broadcast_in_dim x18, other arithmetic, face_slice(): return values[:, :, face_node]  10.8 us
  transfers between devices with their start and end apart: 16, of which 0 were waited for; matrix products, arithmetic and copies ran while one was open for 56% of the time, Pallas kernels for 0%

commit v1 on v0

v1 whole, which is shorter than its diff:
```python
import functools
import math

import jax
import jax.numpy as jnp
import numpy as np
from jax import lax
from jax.experimental import pallas as pl
from jax.experimental.pallas import tpu as pltpu
from jax.sharding import PartitionSpec as P

EZ = 16
DT = 0.02
LIFT = 10.0
METRIC = 2.0
F32 = jnp.float32


WEIGHTS = (1.0 / 10.0, 49.0 / 90.0, 32.0 / 45.0, 49.0 / 90.0, 1.0 / 10.0)


def central_matrix():
    points = np.array([-1.0, -math.sqrt(3.0 / 7.0), 0.0, math.sqrt(3.0 / 7.0), 1.0])
    products = [
        np.prod([points[i] - points[j] for j in range(5) if j != i]) for i in range(5)
    ]
    matrix = np.zeros((5, 5))
    for i in range(5):
        for j in range(5):
            if j != i:
                matrix[i, j] = products[i] / (products[j] * (points[i] - points[j]))
    for i in range(5):
        matrix[i, i] = -np.sum(matrix[i])
    return METRIC * matrix + np.diag([LIFT, 0.0, 0.0, 0.0, -LIFT])


CENTRAL = central_matrix()


def derive(u):
    d = CENTRAL
    e0, e1, m = u[0] + u[4], u[1] + u[3], u[2]
    o0, o1 = u[0] - u[4], u[1] - u[3]
    h = lambda i, j: float(0.5 * (d[i, j] - d[i, 4 - j]))
    g = lambda i, j: float(0.5 * (d[i, j] + d[i, 4 - j]))
    s0 = h(0, 0) * o0 + h(0, 1) * o1
    s1 = h(1, 0) * o0 + h(1, 1) * o1
    d0 = g(0, 0) * e0 + g(0, 1) * e1 + float(d[0, 2]) * m
    d1 = g(1, 0) * e0 + g(1, 1) * e1 + float(d[1, 2]) * m
    mid = float(d[2, 0]) * o0 + float(d[2, 1]) * o1
    return [s0 + d0, s1 + d1, mid, s1 - d1, s0 - d0]


def swap4(x):
    return pltpu.roll(x, 4, 0)


def iotas():
    row = lax.broadcasted_iota(jnp.int32, (8, 128), 0)
    lane = lax.broadcasted_iota(jnp.int32, (8, 128), 1)
    return row, lane


def rows(row, v0, v1, v2, v3):
    return jnp.where(row < 2, v0, jnp.where(row < 4, v1, jnp.where(row < 6, v2, v3)))


class Cells:
    def __init__(self, row, lane):
        self.even = (row & 1) == 0
        self.y_last = lane >= 112
        self.y_first = lane < 16
        self.z_last = (lane & 15) == 15
        self.z_first = (lane & 15) == 0

    def other_half(self, x):
        return jnp.where(self.even, pltpu.roll(x, 7, 0), pltpu.roll(x, 1, 0))

    def y_up(self, x):
        x = pltpu.roll(x, 112, 1)
        return jnp.where(self.y_last, self.other_half(x), x)

    def y_down(self, x):
        x = pltpu.roll(x, 16, 1)
        return jnp.where(self.y_first, self.other_half(x), x)

    def z_up(self, x):
        return jnp.where(self.z_last, pltpu.roll(x, 15, 1), pltpu.roll(x, 127, 1))

    def z_down(self, x):
        return jnp.where(self.z_first, pltpu.roll(x, 113, 1), pltpu.roll(x, 1, 1))


def weight(i, inverse=False):
    w = [1.0 / v if inverse else v for v in WEIGHTS]
    return jnp.where((i == 0) | (i == 4), w[0], jnp.where(i == 2, w[2], w[1])).astype(F32)


def penalty(inner, outer):
    return swap4(LIFT * (outer - inner))


def x_pass(s, t_ref, m_t, ext):
    def body(b, carry):
        for c in range(5):
            n = [25 * a + 5 * b + c for a in range(5)]
            y = [s[1, n[a]] * m_t for a in range(5)]
            z = [s[2, n[a]] * m_t for a in range(5)]
            dy, dz = derive(y), derive(z)
            for a in range(5):
                out_y, out_z = -dz[a], dy[a]
                if a in (0, 4):
                    out_y = out_y - swap4(LIFT * y[a])
                    out_z = out_z - swap4(LIFT * z[a])
                    if ext is not None:
                        more_y, more_z = ext(a, 5 * b + c)
                        out_y, out_z = out_y + more_y, out_z + more_z
                t_ref[1, n[a]] = out_y
                t_ref[2, n[a]] = out_z
        return carry

    lax.fori_loop(0, 5, body, 0)


def y_pass(s, t_ref, m_t, cells):
    def body(a, carry):
        for c in range(5):
            n = [25 * a + 5 * b + c for b in range(5)]
            z = [s[2, n[b]] * m_t for b in range(5)]
            x = [s[0, n[b]] * m_t for b in range(5)]
            dz, dx = derive(z), derive(x)
            for b in range(5):
                out_x = dz[b]
                out_z = t_ref[2, n[b]] - dx[b]
                if b == 0:
                    oz, ox = cells.y_down(z[4]), cells.y_down(x[4])
                    out_x = out_x - LIFT * oz + penalty(x[0], ox)
                    out_z = out_z + LIFT * ox + penalty(z[0], oz)
                if b == 4:
                    oz, ox = cells.y_up(z[0]), cells.y_up(x[0])
                    out_x = out_x + LIFT * oz + penalty(x[4], ox)
                    out_z = out_z - LIFT * ox + penalty(z[4], oz)
                t_ref[0, n[b]] = out_x
                t_ref[2, n[b]] = out_z
        return carry

    lax.fori_loop(0, 5, body, 0)


def z_pass(s, t_ref, m_t, m_s, m_f, cells, out, carry):
    def body(a, carry):
        for b in range(5):
            n = [25 * a + 5 * b + c for c in range(5)]
            s_x = [s[0, n[c]] for c in range(5)]
            s_y = [s[1, n[c]] for c in range(5)]
            x = [v * m_t for v in s_x]
            y = [v * m_t for v in s_y]
            dx, dy = derive(x), derive(y)
            for c in range(5):
                out_y = t_ref[1, n[c]] + dx[c]
                out_x = t_ref[0, n[c]] - dy[c]
                if c == 0:
                    ox, oy = cells.z_down(x[4]), cells.z_down(y[4])
                    out_y = out_y - LIFT * ox + penalty(y[0], oy)
                    out_x = out_x + LIFT * oy + penalty(x[0], ox)
                if c == 4:
                    ox, oy = cells.z_up(x[0]), cells.z_up(y[0])
                    out_y = out_y + LIFT * ox + penalty(y[4], oy)
                    out_x = out_x - LIFT * oy + penalty(x[4], ox)
                for comp, old, got in (
                    (0, s_x[c], out_x),
                    (1, s_y[c], out_y),
                    (2, s[2, n[c]], t_ref[2, n[c]]),
                ):
                    inc = swap4(got) * m_f + old * m_s
                    carry = out(comp, a, b, c, n[c], old, inc, carry)
        return carry

    return lax.fori_loop(0, 5, body, carry)


def materials(perm_ref, reg_ref, cond_ref):
    two = lambda x: jnp.concatenate([x, x, x, x], axis=0)
    perm = perm_ref[...]
    reg = reg_ref[...]
    damping = jnp.zeros((2, 128), F32)
    for r in range(8):
        damping = jnp.where(reg == r, cond_ref[r], damping)
    coef = DT / perm
    return two(coef), two(damping)


def masks(parity, row, coef, damping):
    if parity == 1:
        m_t = rows(row, 1.0, coef, -1.0, 0.0)
        m_f = rows(row, 0.0, 1.0, -DT, 1.0)
        m_s = rows(row, 0.0, -damping * coef, 0.0, 0.0)
    else:
        m_t = rows(row, 1.0, 0.0, 1.0, DT)
        m_f = rows(row, coef, -1.0, 0.0, 1.0)
        m_s = rows(row, -damping * coef, 0.0, 0.0, 0.0)
    return m_t, m_f, m_s


def first_traces(s, lo_ref, hi_ref, m_t, row):
    def body(b, carry):
        for c in range(5):
            k = 5 * b + c
            for a, sign, ref in ((0, 1.0, lo_ref), (4, -1.0, hi_ref)):
                y, z = s[1, 25 * a + k] * m_t, s[2, 25 * a + k] * m_t
                ref[0, k] = jnp.where(row < 2, sign * z - swap4(y), y)
                ref[1, k] = jnp.where(row < 2, -sign * y - swap4(z), z)
        return carry

    lax.fori_loop(0, 5, body, 0)


def second_traces(s, lo_ref, hi_ref, row):
    def body(b, carry):
        for c in range(5):
            k = 5 * b + c
            for a, sign, ref in ((0, 1.0, lo_ref), (4, -1.0, hi_ref)):
                y, z = s[1, 25 * a + k], s[2, 25 * a + k]
                out_y = jnp.where(row < 6, swap4(y) - sign * z, DT * y)
                out_z = jnp.where(row < 6, swap4(z) + sign * y, DT * z)
                ref[0, k] = jnp.where(row < 4, ref[0, k], out_y)
                ref[1, k] = jnp.where(row < 4, ref[1, k], out_z)
        return carry

    lax.fori_loop(0, 5, body, 0)


def odd_level(s, t_ref, lo_ref, hi_ref, row, coef, damping, cells):
    m_t, m_f, m_s = masks(1, row, coef, damping)
    first_traces(s, lo_ref, hi_ref, m_t, row)
    x_pass(s, t_ref, m_t, None)
    y_pass(s, t_ref, m_t, cells)

    def out(comp, a, b, c, n, old, inc, carry):
        s[comp, n] = old + inc
        return carry

    z_pass(s, t_ref, m_t, m_s, m_f, cells, out, 0)
    second_traces(s, lo_ref, hi_ref, row)


def outer_parts(s_in, s, below, above, lo_own, hi_own, row, coef, damping):
    position, last = lax.axis_index("space"), lax.axis_size("space") - 1
    has = {0: (position > 0).astype(F32), 4: (position < last).astype(F32)}
    to_same = rows(row, 0.0, LIFT, 0.0, 0.0)
    to_primal = rows(row, 0.0, 0.0, LIFT * DT, 0.0)
    to_dual = rows(row, 0.0, 0.0, 0.0, LIFT)
    level_two = row >= 4
    late_primal = rows(row, 0.0, 0.0, LIFT, 0.0)
    late_dual = rows(row, 0.0, 0.0, 0.0, LIFT)
    fix = rows(row, -LIFT * DT, LIFT * DT, 0.0, 0.0)
    sides = ((0, -1.0, below, lo_own), (4, 1.0, above, hi_own))

    def body(b, carry):
        for c in range(5):
            k = 5 * b + c
            for a, sign, got, own in sides:
                y, z = got[0, k] * has[a], got[1, k] * has[a]
                ry, rz = swap4(y), swap4(z)
                n = 25 * a + k
                s[1, n] = s_in[1, n] + (ry * to_primal - sign * (rz * to_dual) + y * to_same)
                s[2, n] = s_in[2, n] + (rz * to_primal + sign * (ry * to_dual) + z * to_same)
        return carry

    lax.fori_loop(0, 5, body, 0)

    def ext(a, k):
        _, sign, got, own = sides[0 if a == 0 else 1]
        y = (got[0, k] + sign * swap4(own[1, k] * fix)) * has[a]
        z = (got[1, k] - sign * swap4(own[0, k] * fix)) * has[a]
        ext_y = y * late_primal - sign * (z * late_dual) + swap4(y * late_dual)
        ext_z = z * late_primal + sign * (y * late_dual) + swap4(z * late_dual)
        return ext_y, ext_z

    return ext


def add_source(s, step, layer_ref, cell_ref, node_ref, amp_ref, row, lane, coef):
    here = layer_ref[0] == lax.axis_index("space")
    cell = cell_ref[0]
    node = node_ref[0]
    place = (row < 2) & ((row & 1) * 128 + lane == cell)
    shape = jnp.where(place, coef, 0.0)
    incs = []
    for comp in range(3):
        inc = shape * jnp.where(here, amp_ref[0, 3 * step + comp], 0.0)
        s[comp, node] = s[comp, node] + inc
        incs.append(inc)
    return node, incs


def first_kernel(
    fields, cot, perm_ref, reg_ref, cond_ref, s, lo_ref, hi_ref, t_ref, sems
):
    row, lane = iotas()
    cells = Cells(row, lane)
    copies = [
        pltpu.make_async_copy(src, s.at[:, :, pl.ds(2 * i, 2), :], sems.at[i])
        for i, src in enumerate(
            (fields.at[0:3], cot.at[0:3], fields.at[3:6], cot.at[3:6])
        )
    ]
    for copy in copies:
        copy.start()
    coef, damping = materials(perm_ref, reg_ref, cond_ref)
    for copy in copies:
        copy.wait()
    dual = (row & 2) != 0

    def scale(a, carry):
        for b in range(5):
            for c in range(5):
                n = 25 * a + 5 * b + c
                w = weight(a, True) * (1.0 / (WEIGHTS[b] * WEIGHTS[c]))
                m = jnp.where(dual, w, 1.0)
                for comp in range(3):
                    s[comp, n] = s[comp, n] * m
        return carry

    lax.fori_loop(0, 5, scale, 0)
    odd_level(s, t_ref, lo_ref, hi_ref, row, coef, damping, cells)


def copy_state(s_in, s):
    def body(a, carry):
        for k in range(25):
            for comp in range(3):
                s[comp, 25 * a + k] = s_in[comp, 25 * a + k]
        return carry

    lax.fori_loop(0, 5, body, 0)


def second_kernel(
    s_in, lo_own, hi_own, below, above, perm_ref, reg_ref, cond_ref, layer_ref,
    cell_ref, node_ref, amp_ref, s, lo_ref, hi_ref, g_ref, t_ref,
):
    row, lane = iotas()
    cells = Cells(row, lane)
    coef, damping = materials(perm_ref, reg_ref, cond_ref)
    copy_state(s_in, s)
    ext = outer_parts(s_in, s, below, above, lo_own, hi_own, row, coef, damping)
    m_t, m_f, m_s = masks(2, row, coef, damping)
    x_pass(s, t_ref, m_t, ext)
    y_pass(s, t_ref, m_t, cells)

    def out(comp, a, b, c, n, old, inc, carry):
        new = old + inc
        s[comp, n] = new
        w = weight(a) * (WEIGHTS[b] * WEIGHTS[c])
        return carry + pltpu.roll(inc, 2, 0) * (new * w)

    total = z_pass(s, t_ref, m_t, m_s, m_f, cells, out, jnp.zeros((8, 128), F32))
    node, incs = add_source(
        s, 0, layer_ref, cell_ref, node_ref, amp_ref, row, lane, coef
    )
    w = weight(node // 25) * weight((node // 5) % 5) * weight(node % 5)
    for comp in range(3):
        total = total + pltpu.roll(incs[comp], 2, 0) * (s[comp, node] * w)
    g_ref[...] = total
    odd_level(s, t_ref, lo_ref, hi_ref, row, coef, damping, cells)


def third_kernel(
    s_in, lo_own, hi_own, below, above, perm_ref, reg_ref, cond_ref, layer_ref,
    cell_ref, node_ref, amp_ref, g_in, cot, adj, g_ref, s, t_ref, c_ref, sems,
):
    row, lane = iotas()
    cells = Cells(row, lane)
    load = pltpu.make_async_copy(cot.at[0:3], c_ref.at[:, :, pl.ds(0, 2), :], sems.at[0])
    load.start()
    coef, damping = materials(perm_ref, reg_ref, cond_ref)
    copy_state(s_in, s)
    ext = outer_parts(s_in, s, below, above, lo_own, hi_own, row, coef, damping)
    m_t, m_f, m_s = masks(2, row, coef, damping)
    x_pass(s, t_ref, m_t, ext)
    y_pass(s, t_ref, m_t, cells)
    load.wait()
    dual = (row & 2) != 0

    def out(comp, a, b, c, n, old, inc, carry):
        w = weight(a) * (WEIGHTS[b] * WEIGHTS[c])
        s[comp, n] = (old + inc) * w
        return carry + inc[0:2] * c_ref[comp, n, 0:2]

    total = z_pass(s, t_ref, m_t, m_s, m_f, cells, out, jnp.zeros((2, 128), F32))
    stores = [
        pltpu.make_async_copy(
            s.at[:, :, pl.ds(2 + 4 * i, 2), :], adj.at[3 * i : 3 * i + 3], sems.at[1 + i]
        )
        for i in range(2)
    ]
    for store in stores:
        store.start()
    here = layer_ref[0] == lax.axis_index("space")
    node = node_ref[0]
    place = (row & 1) * 128 + lane == cell_ref[0]
    shape = jnp.where(place, coef, 0.0)[0:2]
    for comp in range(3):
        amp = jnp.where(here, amp_ref[0, 3 + comp], 0.0)
        total = total + (shape * amp) * c_ref[comp, node, 0:2]
    total = total + g_in[2:4]
    g_ref[...] = -total / perm_ref[...]
    for store in stores:
        store.wait()


def struct(*shape):
    return jax.ShapeDtypeStruct(shape, F32)


VMEM = pl.BlockSpec(memory_space=pltpu.VMEM)
SMEM = pl.BlockSpec(memory_space=pltpu.SMEM)
ANY = pl.BlockSpec(memory_space=pl.ANY)
PARAMS = pltpu.CompilerParams(vmem_limit_bytes=24 * 1024 * 1024)
STATE = (3, 125, 8, 128)
TRACE = (2, 25, 8, 128)


def exchange(lo, hi):
    peers = lax.axis_size("space")
    up = [(i, (i + 1) % peers) for i in range(peers)]
    down = [((i + 1) % peers, i) for i in range(peers)]
    below = lax.ppermute(hi, "space", up)
    above = lax.ppermute(lo, "space", down)
    return below, above


def src_sum(x):
    for group in ((1, 2, 3), (4, 8, 12)):
        got = [lax.ppermute(x, "src", [(i, i ^ d) for i in range(16)]) for d in group]
        x = (x + got[0]) + (got[1] + got[2])
    return x


def on_device(
    fields, cotangent, permittivity, regions, conductance, src_layer, src_cell, src_node, src_amp
):
    wide = fields.shape[:2] + (2, 128)
    f = fields.reshape(wide)
    cot = cotangent.reshape(wide)
    perm = permittivity.reshape(2, 128)
    reg = regions.reshape(2, 128)
    material = (perm, reg, conductance)
    source = (src_layer, src_cell, src_node, src_amp)
    s, lo, hi = pl.pallas_call(
        first_kernel,
        out_shape=(struct(*STATE), struct(*TRACE), struct(*TRACE)),
        in_specs=[ANY, ANY, VMEM, VMEM, SMEM],
        out_specs=[VMEM] * 3,
        scratch_shapes=[pltpu.VMEM(STATE, F32), pltpu.SemaphoreType.DMA((4,))],
        compiler_params=PARAMS,
        name="first",
    )(f, cot, *material)
    below, above = exchange(lo, hi)
    s, lo, hi, g = pl.pallas_call(
        second_kernel,
        out_shape=(struct(*STATE), struct(*TRACE), struct(*TRACE), struct(8, 128)),
        in_specs=[VMEM] * 7 + [SMEM] * 5,
        out_specs=[VMEM] * 4,
        scratch_shapes=[pltpu.VMEM(STATE, F32)],
        compiler_params=PARAMS,
        name="second",
    )(s, lo, hi, below, above, *material, *source)
    below, above = exchange(lo, hi)
    adjoint, g = pl.pallas_call(
        third_kernel,
        out_shape=(struct(*wide), struct(2, 128)),
        in_specs=[VMEM] * 7 + [SMEM] * 5 + [VMEM, ANY],
        out_specs=[ANY, VMEM],
        scratch_shapes=[
            pltpu.VMEM(STATE, F32),
            pltpu.VMEM(STATE, F32),
            pltpu.VMEM(STATE, F32),
            pltpu.SemaphoreType.DMA((3,)),
        ],
        compiler_params=PARAMS,
        name="third",
    )(s, lo, hi, below, above, *material, *source, g, cot)
    gradient = src_sum(g).reshape(permittivity.shape)
    return adjoint.reshape(fields.shape), gradient


def solution(mesh):
    return jax.shard_map(
        on_device,
        mesh=mesh,
        in_specs=(
            P(None, None, "src", "space", None),
            P(None, None, "src", "space", None),
            P("space", None),
            P("space", None),
            P(),
            P("src"),
            P("src"),
            P("src"),
            P("src", None),
        ),
        out_specs=(P(None, None, "src", "space", None), P("space", None)),
        check_vma=False,
    )
```

time: 329 us -> 65.1 us (0.20)
  the two profiles are of different devices: /device:TPU:89 before, /device:TPU:1 now
where the time goes in v1:
time: 65.1 us; the launch traced here: 64.9 us
  waiting for transfers between devices  25.7 us (39%)
  starting transfers between devices  19.3 us (30%)
  Pallas kernels  10.3 us (16%)
  local copies, waits for them, and re-layouts  6.45 us (10%)
  between operations  2.65 us (4%)
    ppermute x2, waiting for transfers between devices, exchange(): above = lax.ppermute(lo, 'space', down)  11.6 us
    ppermute x2, waiting for transfers between devices, exchange(): below = lax.ppermute(hi, 'space', up)  11.1 us
    ppermute x2, starting transfers between devices, exchange(): above = lax.ppermute(lo, 'space', down)  10.3 us
    ppermute x6, starting transfers between devices, src_sum(): lax.ppermute(x, 'src', [(i, i ^ d) for i in range(16)])  8.35 us
    unnamed x15, local copies, waits for them, and re-layouts  6.02 us
    pallas_call x1, Pallas kernels, on_device(): pl.pallas_call(second_kernel, out_shape=(struct(*STATE), struct(*TRACE),...  4.29 us
    pallas_call x1, Pallas kernels, on_device(): pl.pallas_call(third_kernel, out_shape=(struct(*wide), struct(2, 128)), i...  3.08 us
    ppermute x6, waiting for transfers between devices, src_sum(): lax.ppermute(x, 'src', [(i, i ^ d) for i in range(16)])  2.89 us
  transfers between devices with their start and end apart: 10, of which 7 were waited for; matrix products, arithmetic and copies ran while one was open for 3% of the time, Pallas kernels for 0%

profile of v1, /device:TPU:1, one launch (start us, length us, event | category | flops | bytes accessed | tf_op | source)
XLA Modules:
  0.0 64.9 jit_solution(2181366326549318449)
XLA Ops:
  0.6 0.0 copy-start
  0.7 1.1 %copy-done = f32[6,125,1,1,256]{4,3,2,1,0:T(1,128)S(1)} copy-done((f32[6,125,1,1,256]{4,3,2,1,0:T(1,128)S(1)}, f32[6,125,1,1,256]{4,3,2,1,0:T(1,128)}, u32[]{:S(2)}) %copy-start) | copy-done | bytes 768024
  1.8 1.1 %copy-done.2 = f32[6,125,1,1,256]{4,3,2,1,0:T(1,128)S(1)} copy-done((f32[6,125,1,1,256]{4,3,2,1,0:T(1,128)S(1)}, f32[6,125,1,1,256]{4,3,2,1,0:T(1,128)}, u32[]{:S(2)}) %copy-start.2) | copy-done | bytes 768024
  2.9 0.7 %copy-done.3 = f32[1,256]{1,0:T(1,128)S(1)} copy-done((f32[1,256]{1,0:T(1,128)S(1)}, f32[1,256]{1,0:T(1,128)}, u32[]{:S(2)}) %copy-start.3) | copy-done | bytes 1048
  3.6 0.7 %copy-done.4 = s32[1,256]{1,0:T(1,128)S(1)} copy-done((s32[1,256]{1,0:T(1,128)S(1)}, s32[1,256]{1,0:T(1,128)}, u32[]{:S(2)}) %copy-start.4) | copy-done | bytes 1048
  4.3 0.7 %copy-done.5 = f32[8]{0:T(128)S(1)} copy-done((f32[8]{0:T(128)S(1)}, f32[8]{0:T(128)}, u32[]{:S(2)}) %copy-start.5) | copy-done | bytes 56
  4.9 2.9 %first.1 = (f32[3,125,8,128]{3,2,1,0:T(8,128)S(1)}, f32[2,25,8,128]{3,2,1,0:T(8,128)S(1)}, f32[2,25,8,128]{3,2,1,0:T(8,128)S(1)}) custom-call(f32[6,125,2,128]{3,2,1,0:T(2,128)S(1)} %bitcast.8, f32[6,125,2,128]{3,2,1,0:T(2,128)S(1)} %bitcast.6, f32[2,128]{1,0:T(2,128)S(1)} %bitcast.9, s32[2,128]{1,0:T(2,128)S(1)} %bitcast.12, f32[8]{0:T(128)S(1)} %copy-done.5), custom_call_target="tpu_custom_call" | custom-call | tf_op jit(solution)/shard_map/first/pallas_call | solution.py:451
  7.8 0.0 copy-start.1
  7.8 9.4 %collective-permute-start.1 = (f32[2,25,8,128]{3,2,1,0:T(8,128)S(1)}, f32[2,25,8,128]{3,2,1,0:T(8,128)S(1)}, u32[]{:S(2)}, u32[]{:S(2)}) collective-permute-start(f32[2,25,8,128]{3,2,1,0:T(8,128)S(1)} %get-tuple-element.12.lo_own), channel_id=1, source_target_pairs={{16,0},{32,16},{48,32},{64,48},{80,64},{96,80},{112,96},{128,112},... | collective-permute-start | bytes 614408 | tf_op jit(solution)/shard_map/ppermute | solution.py:430
  17.2 0.0 collective-permute-start
  19.1 3.4 %collective-permute-done.1.above = f32[2,25,8,128]{3,2,1,0:T(8,128)S(1)} collective-permute-done((f32[2,25,8,128]{3,2,1,0:T(8,128)S(1)}, f32[2,25,8,128]{3,2,1,0:T(8,128)S(1)}, u32[]{:S(2)}, u32[]{:S(2)}) %collective-permute-start.1) | collective-permute-done | bytes 204832 | tf_op jit(solution)/shard_map/ppermute | solution.py:430
  22.6 8.4 %collective-permute-done.below = f32[2,25,8,128]{3,2,1,0:T(8,128)S(1)} collective-permute-done((f32[2,25,8,128]{3,2,1,0:T(8,128)S(1)}, f32[2,25,8,128]{3,2,1,0:T(8,128)S(1)}, u32[]{:S(2)}, u32[]{:S(2)}) %collective-permute-start) | collective-permute-done | bytes 204832 | tf_op jit(solution)/shard_map/ppermute | solution.py:429
  31.0 4.3 %second.1 = (f32[3,125,8,128]{3,2,1,0:T(8,128)S(1)}, f32[2,25,8,128]{3,2,1,0:T(8,128)S(1)}, f32[2,25,8,128]{3,2,1,0:T(8,128)S(1)}, f32[8,128]{1,0:T(8,128)S(1)}) custom-call(f32[3,125,8,128]{3,2,1,0:T(8,128)S(1)} %get-tuple-element.11.s_in, f32[2,25,8,128]{3,2,1,0:T(8,128)S(1)} %get-tuple-element.12.lo_own, f32[2,25,8,128]{3,2,1,0:T(8,128)S(1)} %get-tuple-element.13.hi_own, ...), custom_call_target="tpu_custom_call" | custom-call | tf_op jit(solution)/shard_map/second/pallas_call | solution.py:461
  35.3 0.9 %collective-permute-start.3 = (f32[2,25,8,128]{3,2,1,0:T(8,128)S(1)}, f32[2,25,8,128]{3,2,1,0:T(8,128)S(1)}, u32[]{:S(2)}, u32[]{:S(2)}) collective-permute-start(f32[2,25,8,128]{3,2,1,0:T(8,128)S(1)} %get-tuple-element.15.lo_own), channel_id=1, source_target_pairs={{16,0},{32,16},{48,32},{64,48},{80,64},{96,80},{112,96},{128,112},... | collective-permute-start | bytes 614408 | tf_op jit(solution)/shard_map/ppermute | solution.py:430
  36.2 0.6 collective-permute-start.2
  36.8 8.2 %collective-permute-done.3.above = f32[2,25,8,128]{3,2,1,0:T(8,128)S(1)} collective-permute-done((f32[2,25,8,128]{3,2,1,0:T(8,128)S(1)}, f32[2,25,8,128]{3,2,1,0:T(8,128)S(1)}, u32[]{:S(2)}, u32[]{:S(2)}) %collective-permute-start.3) | collective-permute-done | bytes 204832 | tf_op jit(solution)/shard_map/ppermute | solution.py:430
  45.0 2.7 %collective-permute-done.2.below = f32[2,25,8,128]{3,2,1,0:T(8,128)S(1)} collective-permute-done((f32[2,25,8,128]{3,2,1,0:T(8,128)S(1)}, f32[2,25,8,128]{3,2,1,0:T(8,128)S(1)}, u32[]{:S(2)}, u32[]{:S(2)}) %collective-permute-start.2) | collective-permute-done | bytes 204832 | tf_op jit(solution)/shard_map/ppermute | solution.py:429
  47.8 3.1 %third.1 = (f32[6,125,2,128]{3,2,1,0:T(2,128)S(1)}, f32[2,128]{1,0:T(2,128)S(1)}) custom-call(f32[3,125,8,128]{3,2,1,0:T(8,128)S(1)} %get-tuple-element.14.s_in, f32[2,25,8,128]{3,2,1,0:T(8,128)S(1)} %get-tuple-element.15.lo_own, f32[2,25,8,128]{3,2,1,0:T(8,128)S(1)} %get-tuple-element.16.hi_own, f32[2,25,8,128]{3,2,1,0:T(8,128)S(1)} %collective-permute-done.2.below, ...), custom_call_target="tpu_custom_call" | custom-call | tf_op jit(solution)/shard_map/third/pallas_call | solution.py:471
  50.9 4.5 %collective-permute-start.6 = (f32[2,128]{1,0:T(2,128)S(1)}, f32[2,128]{1,0:T(2,128)S(1)}, u32[]{:S(2)}, u32[]{:S(2)}) collective-permute-start(f32[2,128]{1,0:T(2,128)S(1)} %get-tuple-element.19), channel_id=1, source_target_pairs={{0,3},{1,2},{2,1},{3,0},{4,7},{5,6},{6,5},{7,4},{8,11},{9,10},{10,... | collective-permute-start | bytes 3080 | tf_op jit(solution)/shard_map/ppermute | solution.py:436
  55.4 0.0 collective-permute-start.5
  55.4 0.5 collective-permute-start.4
  55.9 0.8 %collective-permute-done.6 = f32[2,128]{1,0:T(2,128)S(1)} collective-permute-done((f32[2,128]{1,0:T(2,128)S(1)}, f32[2,128]{1,0:T(2,128)S(1)}, u32[]{:S(2)}, u32[]{:S(2)}) %collective-permute-start.6) | collective-permute-done | bytes 1056 | tf_op jit(solution)/shard_map/ppermute | solution.py:436
  56.6 1.2 %collective-permute-done.5 = f32[2,128]{1,0:T(2,128)S(1)} collective-permute-done((f32[2,128]{1,0:T(2,128)S(1)}, f32[2,128]{1,0:T(2,128)S(1)}, u32[]{:S(2)}, u32[]{:S(2)}) %collective-permute-start.5) | collective-permute-done | bytes 1056 | tf_op jit(solution)/shard_map/ppermute | solution.py:436
  57.8 0.0 collective-permute-done.4
  57.8 2.6 %collective-permute-start.9 = (f32[2,128]{1,0:T(2,128)S(1)}, f32[2,128]{1,0:T(2,128)S(1)}, u32[]{:S(2)}, u32[]{:S(2)}) collective-permute-start(f32[2,128]{1,0:T(2,128)S(1)} %add_add_fusion.1), channel_id=1, source_target_pairs={{0,12},{1,13},{2,14},{3,15},{4,8},{5,9},{6,10},{7,11},{8,4},{9,5},... | collective-permute-start | bytes 3080 | tf_op jit(solution)/shard_map/ppermute | solution.py:436
  60.4 0.5 collective-permute-start.8
  60.9 0.3 collective-permute-start.7
  61.2 0.4 copy.12
  61.6 1.7 %copy.13 = f32[6,125,1,1,256]{4,3,2,1,0:T(1,128)} copy(f32[6,125,1,1,256]{1,4,0,3,2:T(8,128)S(1)} %bitcast.15) | data formatting | bytes 1536000
  63.3 0.0 collective-permute-done.9
  63.3 1.0 %collective-permute-done.8 = f32[2,128]{1,0:T(2,128)S(1)} collective-permute-done((f32[2,128]{1,0:T(2,128)S(1)}, f32[2,128]{1,0:T(2,128)S(1)}, u32[]{:S(2)}, u32[]{:S(2)}) %collective-permute-start.8) | collective-permute-done | bytes 1056 | tf_op jit(solution)/shard_map/ppermute | solution.py:436
  64.3 0.6 add_add_fusion
  (9 shorter events, 0.0 us)
Async XLA Ops:
  0.6 30.4 %copy-start.6 = (f32[1,6]{1,0:T(1,128)S(1)}, f32[1,6]{1,0:T(1,128)}, u32[]{:S(2)}) copy-start(f32[1,6]{1,0:T(1,128)} %amp_ref.3) | copy-start | bytes 76
  0.6 1.1 %copy-start = (f32[6,125,1,1,256]{4,3,2,1,0:T(1,128)S(1)}, f32[6,125,1,1,256]{4,3,2,1,0:T(1,128)}, u32[]{:S(2)}) copy-start(f32[6,125,1,1,256]{4,3,2,1,0:T(1,128)} %param.10) | copy-start | bytes 2304004
  1.8 1.1 %copy-start.2 = (f32[6,125,1,1,256]{4,3,2,1,0:T(1,128)S(1)}, f32[6,125,1,1,256]{4,3,2,1,0:T(1,128)}, u32[]{:S(2)}) copy-start(f32[6,125,1,1,256]{4,3,2,1,0:T(1,128)} %param.9) | copy-start | bytes 2304004
  2.9 0.7 %copy-start.3 = (f32[1,256]{1,0:T(1,128)S(1)}, f32[1,256]{1,0:T(1,128)}, u32[]{:S(2)}) copy-start(f32[1,256]{1,0:T(1,128)} %param.11) | copy-start | bytes 3076
  3.6 0.7 %copy-start.4 = (s32[1,256]{1,0:T(1,128)S(1)}, s32[1,256]{1,0:T(1,128)}, u32[]{:S(2)}) copy-start(s32[1,256]{1,0:T(1,128)} %param.12) | copy-start | bytes 3076
  4.3 0.7 %copy-start.5 = (f32[8]{0:T(128)S(1)}, f32[8]{0:T(128)}, u32[]{:S(2)}) copy-start(f32[8]{0:T(128)} %cond_ref.5) | copy-start | bytes 100
  7.8 40.0 %copy-start.1 = (f32[6,125,1,1,256]{4,3,2,1,0:T(1,128)S(1)}, f32[6,125,1,1,256]{4,3,2,1,0:T(1,128)}, u32[]{:S(2)}) copy-start(f32[6,125,1,1,256]{4,3,2,1,0:T(1,128)} %param.10) | copy-start | bytes 2304004
  7.8 14.8 %collective-permute-start.1 = (f32[2,25,8,128]{3,2,1,0:T(8,128)S(1)}, f32[2,25,8,128]{3,2,1,0:T(8,128)S(1)}, u32[]{:S(2)}, u32[]{:S(2)}) collective-permute-start(f32[2,25,8,128]{3,2,1,0:T(8,128)S(1)} %get-tuple-element.12.lo_own), channel_id=1, source_target_pairs={{16,0},{32,16},{48,32},{64,48},{80,64},{96,80},{112,96},{128,112},... | collective-permute-start | bytes 614408 | tf_op jit(solution)/shard_map/ppermute | solution.py:430
  17.2 13.8 %collective-permute-start = (f32[2,25,8,128]{3,2,1,0:T(8,128)S(1)}, f32[2,25,8,128]{3,2,1,0:T(8,128)S(1)}, u32[]{:S(2)}, u32[]{:S(2)}) collective-permute-start(f32[2,25,8,128]{3,2,1,0:T(8,128)S(1)} %get-tuple-element.13.hi_own), channel_id=1, source_target_pairs={{0,16},{16,32},{32,48},{48,64},{64,80},{80,96},{96,112},{112,128},... | collective-permute-start | bytes 614408 | tf_op jit(solution)/shard_map/ppermute | solution.py:429
  35.3 9.7 %collective-permute-start.3 = (f32[2,25,8,128]{3,2,1,0:T(8,128)S(1)}, f32[2,25,8,128]{3,2,1,0:T(8,128)S(1)}, u32[]{:S(2)}, u32[]{:S(2)}) collective-permute-start(f32[2,25,8,128]{3,2,1,0:T(8,128)S(1)} %get-tuple-element.15.lo_own), channel_id=1, source_target_pairs={{16,0},{32,16},{48,32},{64,48},{80,64},{96,80},{112,96},{128,112},... | collective-permute-start | bytes 614408 | tf_op jit(solution)/shard_map/ppermute | solution.py:430
  36.2 11.6 %collective-permute-start.2 = (f32[2,25,8,128]{3,2,1,0:T(8,128)S(1)}, f32[2,25,8,128]{3,2,1,0:T(8,128)S(1)}, u32[]{:S(2)}, u32[]{:S(2)}) collective-permute-start(f32[2,25,8,128]{3,2,1,0:T(8,128)S(1)} %get-tuple-element.16.hi_own), channel_id=1, source_target_pairs={{0,16},{16,32},{32,48},{48,64},{64,80},{80,96},{96,112},{112,128},... | collective-permute-start | bytes 614408 | tf_op jit(solution)/shard_map/ppermute | solution.py:429
  50.9 5.8 %collective-permute-start.6 = (f32[2,128]{1,0:T(2,128)S(1)}, f32[2,128]{1,0:T(2,128)S(1)}, u32[]{:S(2)}, u32[]{:S(2)}) collective-permute-start(f32[2,128]{1,0:T(2,128)S(1)} %get-tuple-element.19), channel_id=1, source_target_pairs={{0,3},{1,2},{2,1},{3,0},{4,7},{5,6},{6,5},{7,4},{8,11},{9,10},{10,... | collective-permute-start | bytes 3080 | tf_op jit(solution)/shard_map/ppermute | solution.py:436
  55.4 2.4 %collective-permute-start.5 = (f32[2,128]{1,0:T(2,128)S(1)}, f32[2,128]{1,0:T(2,128)S(1)}, u32[]{:S(2)}, u32[]{:S(2)}) collective-permute-start(f32[2,128]{1,0:T(2,128)S(1)} %get-tuple-element.19), channel_id=1, source_target_pairs={{0,2},{1,3},{2,0},{3,1},{4,6},{5,7},{6,4},{7,5},{8,10},{9,11},{10,... | collective-permute-start | bytes 3080 | tf_op jit(solution)/shard_map/ppermute | solution.py:436
  55.4 2.4 %collective-permute-start.4 = (f32[2,128]{1,0:T(2,128)S(1)}, f32[2,128]{1,0:T(2,128)S(1)}, u32[]{:S(2)}, u32[]{:S(2)}) collective-permute-start(f32[2,128]{1,0:T(2,128)S(1)} %get-tuple-element.19), channel_id=1, source_target_pairs={{0,1},{1,0},{2,3},{3,2},{4,5},{5,4},{6,7},{7,6},{8,9},{9,8},{10,11... | collective-permute-start | bytes 3080 | tf_op jit(solution)/shard_map/ppermute | solution.py:436
  57.8 5.5 %collective-permute-start.9 = (f32[2,128]{1,0:T(2,128)S(1)}, f32[2,128]{1,0:T(2,128)S(1)}, u32[]{:S(2)}, u32[]{:S(2)}) collective-permute-start(f32[2,128]{1,0:T(2,128)S(1)} %add_add_fusion.1), channel_id=1, source_target_pairs={{0,12},{1,13},{2,14},{3,15},{4,8},{5,9},{6,10},{7,11},{8,4},{9,5},... | collective-permute-start | bytes 3080 | tf_op jit(solution)/shard_map/ppermute | solution.py:436
  60.4 3.9 %collective-permute-start.8 = (f32[2,128]{1,0:T(2,128)S(1)}, f32[2,128]{1,0:T(2,128)S(1)}, u32[]{:S(2)}, u32[]{:S(2)}) collective-permute-start(f32[2,128]{1,0:T(2,128)S(1)} %add_add_fusion.1), channel_id=1, source_target_pairs={{0,8},{1,9},{2,10},{3,11},{4,12},{5,13},{6,14},{7,15},{8,0},{9,1},... | collective-permute-start | bytes 3080 | tf_op jit(solution)/shard_map/ppermute | solution.py:436
  60.9 3.4 %collective-permute-start.7 = (f32[2,128]{1,0:T(2,128)S(1)}, f32[2,128]{1,0:T(2,128)S(1)}, u32[]{:S(2)}, u32[]{:S(2)}) collective-permute-start(f32[2,128]{1,0:T(2,128)S(1)} %add_add_fusion.1), channel_id=1, source_target_pairs={{0,4},{1,5},{2,6},{3,7},{4,0},{5,1},{6,2},{7,3},{8,12},{9,13},{10,... | collective-permute-start | bytes 3080 | tf_op jit(solution)/shard_map/ppermute | solution.py:436

commit v2 on v1

v2 whole, which is shorter than its diff:
```python
import math

import jax
import jax.numpy as jnp
import numpy as np
from jax import lax
from jax.experimental import pallas as pl
from jax.experimental.layout import Layout, with_layout_constraint
from jax.experimental.pallas import tpu as pltpu
from jax.sharding import PartitionSpec as P

EZ = 16
DT = 0.02
LIFT = 10.0
METRIC = 2.0
F32 = jnp.float32


WEIGHTS = (1.0 / 10.0, 49.0 / 90.0, 32.0 / 45.0, 49.0 / 90.0, 1.0 / 10.0)


def central_matrix():
    points = np.array([-1.0, -math.sqrt(3.0 / 7.0), 0.0, math.sqrt(3.0 / 7.0), 1.0])
    products = [
        np.prod([points[i] - points[j] for j in range(5) if j != i]) for i in range(5)
    ]
    matrix = np.zeros((5, 5))
    for i in range(5):
        for j in range(5):
            if j != i:
                matrix[i, j] = products[i] / (products[j] * (points[i] - points[j]))
    for i in range(5):
        matrix[i, i] = -np.sum(matrix[i])
    return (METRIC * matrix + np.diag([LIFT, 0.0, 0.0, 0.0, -LIFT])) / LIFT


CENTRAL = central_matrix()


def halves():
    d = CENTRAL
    h = [[float(0.5 * (d[i, j] - d[i, 4 - j])) for j in range(2)] for i in range(2)]
    g = [[float(0.5 * (d[i, j] + d[i, 4 - j])) for j in range(2)] for i in range(2)]
    return h, g, [float(d[i, 2]) for i in range(2)], [float(d[2, j]) for j in range(2)]


ODD, EVEN, MIDDLE, CENTRE = halves()


def derive(u):
    e0, e1, m = u[0] + u[4], u[1] + u[3], u[2]
    o0, o1 = u[0] - u[4], u[1] - u[3]
    s0 = ODD[0][0] * o0 + ODD[0][1] * o1
    s1 = ODD[1][0] * o0 + ODD[1][1] * o1
    d0 = EVEN[0][0] * e0 + EVEN[0][1] * e1 + MIDDLE[0] * m
    d1 = EVEN[1][0] * e0 + EVEN[1][1] * e1 + MIDDLE[1] * m
    mid = CENTRE[0] * o0 + CENTRE[1] * o1
    return [s0 + d0, s1 + d1, mid, s1 - d1, s0 - d0]


def derive_at_ends(u):
    e0, e1, m = u[0] + u[4], u[1] + u[3], u[2]
    o0, o1 = u[0] - u[4], u[1] - u[3]
    s0 = ODD[0][0] * o0 + ODD[0][1] * o1
    d0 = EVEN[0][0] * e0 + EVEN[0][1] * e1 + MIDDLE[0] * m
    return {0: s0 + d0, 4: s0 - d0}


def derive_inside(u):
    e0, e1, m = u[0] + u[4], u[1] + u[3], u[2]
    o0, o1 = u[0] - u[4], u[1] - u[3]
    s1 = ODD[1][0] * o0 + ODD[1][1] * o1
    d1 = EVEN[1][0] * e0 + EVEN[1][1] * e1 + MIDDLE[1] * m
    mid = CENTRE[0] * o0 + CENTRE[1] * o1
    return {1: s1 + d1, 2: mid, 3: s1 - d1}


def derive_from_inside(u):
    e1, o1, m = u[1] + u[3], u[1] - u[3], u[2]
    s0, s1 = ODD[0][1] * o1, ODD[1][1] * o1
    d0 = EVEN[0][1] * e1 + MIDDLE[0] * m
    d1 = EVEN[1][1] * e1 + MIDDLE[1] * m
    return [s0 + d0, s1 + d1, CENTRE[1] * o1, s1 - d1, s0 - d0]


def derive_from_ends(u0, u4):
    e0, o0 = u0 + u4, u0 - u4
    s0, s1 = ODD[0][0] * o0, ODD[1][0] * o0
    d0, d1 = EVEN[0][0] * e0, EVEN[1][0] * e0
    return [s0 + d0, s1 + d1, CENTRE[0] * o0, s1 - d1, s0 - d0]


def swap4(x):
    return pltpu.roll(x, 4, 0)


def iotas():
    row = lax.broadcasted_iota(jnp.int32, (8, 128), 0)
    lane = lax.broadcasted_iota(jnp.int32, (8, 128), 1)
    return row, lane


def rows(row, v0, v1, v2, v3):
    return jnp.where(row < 2, v0, jnp.where(row < 4, v1, jnp.where(row < 6, v2, v3)))


class Cells:
    def __init__(self, row, lane):
        self.even = (row & 1) == 0
        self.y_last = lane >= 112
        self.y_first = lane < 16
        self.z_last = (lane & 15) == 15
        self.z_first = (lane & 15) == 0

    def other_half(self, x):
        return jnp.where(self.even, pltpu.roll(x, 7, 0), pltpu.roll(x, 1, 0))

    def y_up(self, x):
        x = pltpu.roll(x, 112, 1)
        return jnp.where(self.y_last, self.other_half(x), x)

    def y_down(self, x):
        x = pltpu.roll(x, 16, 1)
        return jnp.where(self.y_first, self.other_half(x), x)

    def z_up(self, x):
        return jnp.where(self.z_last, pltpu.roll(x, 15, 1), pltpu.roll(x, 127, 1))

    def z_down(self, x):
        return jnp.where(self.z_first, pltpu.roll(x, 113, 1), pltpu.roll(x, 1, 1))


ENDS, INSIDE = (0, 4), (1, 2, 3)


def node_weight(a, k):
    return WEIGHTS[a] * WEIGHTS[k // 5] * WEIGHTS[k % 5]


def weight_at(i):
    return jnp.where((i == 0) | (i == 4), WEIGHTS[0], jnp.where(i == 2, WEIGHTS[2], WEIGHTS[1]))


def penalty(inner, outer):
    return swap4(outer - inner)


def y_lines(planes, get, add, cells):
    for a in planes:
        for c in range(5):
            z = [get(2, a, 5 * b + c) for b in range(5)]
            x = [get(0, a, 5 * b + c) for b in range(5)]
            out_x, out_z = derive(z), [-v for v in derive(x)]
            oz, ox = cells.y_down(z[4]), cells.y_down(x[4])
            out_x[0] = out_x[0] - oz + penalty(x[0], ox)
            out_z[0] = out_z[0] + ox + penalty(z[0], oz)
            oz, ox = cells.y_up(z[0]), cells.y_up(x[0])
            out_x[4] = out_x[4] + oz + penalty(x[4], ox)
            out_z[4] = out_z[4] - ox + penalty(z[4], oz)
            for b in range(5):
                add(a, 5 * b + c, out_x[b], out_z[b])


def z_lines(planes, get, add, cells):
    for a in planes:
        for b in range(5):
            x = [get(0, a, 5 * b + c) for c in range(5)]
            y = [get(1, a, 5 * b + c) for c in range(5)]
            out_y, out_x = derive(x), [-v for v in derive(y)]
            ox, oy = cells.z_down(x[4]), cells.z_down(y[4])
            out_y[0] = out_y[0] - ox + penalty(y[0], oy)
            out_x[0] = out_x[0] + oy + penalty(x[0], ox)
            ox, oy = cells.z_up(x[0]), cells.z_up(y[0])
            out_y[4] = out_y[4] + ox + penalty(y[4], oy)
            out_x[4] = out_x[4] - oy + penalty(x[4], ox)
            for c in range(5):
                add(a, 5 * b + c, out_x[c], out_y[c])


def yz_into(planes, get, t, where, cells, final):
    def add_y(a, k, x, z):
        i = where(a, k)
        t[(0, *i)] = x
        t[(2, *i)] = t[(2, *i)] + z

    def add_z(a, k, x, y):
        i = where(a, k)
        final(a, k, t[(0, *i)] + x, t[(1, *i)] + y, t[(2, *i)])

    for a in planes:
        y_lines((a,), get, add_y, cells)
        z_lines((a,), get, add_z, cells)


def masks(parity, row, coef, damping):
    if parity == 1:
        m_t = rows(row, 1.0, coef, -1.0, 0.0)
        m_f = rows(row, 0.0, LIFT, -LIFT * DT, LIFT)
        m_s = rows(row, 0.0, -damping * coef, 0.0, 0.0)
    else:
        m_t = rows(row, 1.0, 0.0, 1.0, DT)
        m_f = rows(row, LIFT * coef, -LIFT, 0.0, LIFT)
        m_s = rows(row, -damping * coef, 0.0, 0.0, 0.0)
    return m_t, m_f, m_s


def materials(perm, reg, cond, aux):
    two = lambda x: jnp.concatenate([x, x, x, x], axis=0)
    perm, reg = perm[...], reg[...]
    damping = jnp.zeros((2, 128), F32)
    for r in range(8):
        damping = jnp.where(reg == r, cond[r], damping)
    coef, damping = two(DT / perm), two(damping)
    aux[0], aux[1] = coef, damping
    return coef, damping


def source_planes(step, layer, cell, amp, row, lane, coef):
    here = layer[0] == lax.axis_index("space")
    place = (row < 2) & ((row & 1) * 128 + lane == cell[0])
    shape = jnp.where(place, coef, 0.0)
    return [shape * jnp.where(here, amp[0, 3 * step + i], 0.0) for i in range(3)]


def end_traces_one(s, lo_ref, hi_ref, m_t, row):
    for k in range(25):
        for a, sign, ref in ((0, 1.0, lo_ref), (4, -1.0, hi_ref)):
            y, z = s[1, 25 * a + k] * m_t, s[2, 25 * a + k] * m_t
            ref[0, k] = jnp.where(row < 2, sign * z - swap4(y), y)
            ref[1, k] = jnp.where(row < 2, -sign * y - swap4(z), z)


def end_traces_two(sf, lo_ref, hi_ref, row):
    for k in range(25):
        for side, sign, ref in ((0, 1.0, lo_ref), (1, -1.0, hi_ref)):
            y, z = sf[1, side, k], sf[2, side, k]
            out_y = jnp.where(row < 6, swap4(y) - sign * z, DT * y)
            out_z = jnp.where(row < 6, swap4(z) + sign * y, DT * z)
            ref[0, k] = jnp.where(row < 4, ref[0, k], out_y)
            ref[1, k] = jnp.where(row < 4, ref[1, k], out_z)


def odd_ends(s, sf, tf, lo_ref, hi_ref, row, coef, damping, cells):
    m_t, m_f, m_s = masks(1, row, coef, damping)
    keep = 1.0 + m_s
    end_traces_one(s, lo_ref, hi_ref, m_t, row)
    get = lambda comp, a, k: s[comp, 25 * a + k] * m_t
    for k in range(25):
        y = [get(1, a, k) for a in range(5)]
        z = [get(2, a, k) for a in range(5)]
        dy, dz = derive_at_ends(y), derive_at_ends(z)
        for a in ENDS:
            tf[1, a // 4, k] = -dz[a] - swap4(y[a])
            tf[2, a // 4, k] = dy[a] - swap4(z[a])

    def final(a, k, *got):
        for comp in range(3):
            sf[comp, a // 4, k] = s[comp, 25 * a + k] * keep + swap4(got[comp]) * m_f

    yz_into(ENDS, get, tf, lambda a, k: (a // 4, k), cells, final)
    end_traces_two(sf, lo_ref, hi_ref, row)


def inner_kernel(s, aux, si, ci):
    row, lane = iotas()
    cells = Cells(row, lane)
    coef, damping = aux[0], aux[1]
    m_t, m_f, m_s = masks(1, row, coef, damping)
    keep = 1.0 + m_s
    get = lambda comp, a, k: s[comp, 25 * a + k] * m_t
    for k in range(25):
        dy = derive_inside([get(1, a, k) for a in range(5)])
        dz = derive_inside([get(2, a, k) for a in range(5)])
        for a in INSIDE:
            ci[1, 25 * a + k] = -dz[a]
            ci[2, 25 * a + k] = dy[a]

    def final(a, k, *got):
        for comp in range(3):
            si[comp, a - 1, k] = s[comp, 25 * a + k] * keep + swap4(got[comp]) * m_f

    whole = lambda a, k: (25 * a + k,)
    yz_into(INSIDE, get, ci, whole, cells, final)
    m_t2, _, _ = masks(2, row, coef, damping)
    get2 = lambda comp, a, k: si[comp, a - 1, k] * m_t2
    for k in range(25):
        dy = derive_from_inside([None] + [get2(1, a, k) for a in INSIDE])
        dz = derive_from_inside([None] + [get2(2, a, k) for a in INSIDE])
        for a in range(5):
            ci[1, 25 * a + k] = -dz[a]
            ci[2, 25 * a + k] = dy[a]

    def store(a, k, *got):
        for comp in range(3):
            ci[comp, 25 * a + k] = got[comp]

    yz_into(INSIDE, get2, ci, whole, cells, store)


def even_half(sf, si, ci, tf, below, above, lo_own, hi_own, row, m_t, cells, final):
    position, last = lax.axis_index("space"), lax.axis_size("space") - 1
    has = {0: (position > 0).astype(F32), 4: (position < last).astype(F32)}
    to_same = rows(row, 0.0, LIFT, 0.0, 0.0)
    to_primal = rows(row, 0.0, 0.0, LIFT * DT, 0.0)
    to_dual = rows(row, 0.0, 0.0, 0.0, LIFT)
    late_primal = rows(row, 0.0, 0.0, 1.0, 0.0)
    late_dual = rows(row, 0.0, 0.0, 0.0, 1.0)
    fix = rows(row, -LIFT * DT, LIFT * DT, 0.0, 0.0)
    for k in range(25):
        ends = {}
        for a, sign, got, own in ((0, -1.0, below, lo_own), (4, 1.0, above, hi_own)):
            y, z = got[0, k] * has[a], got[1, k] * has[a]
            ry, rz = swap4(y), swap4(z)
            s_y = sf[1, a // 4, k] + (ry * to_primal - sign * (rz * to_dual) + y * to_same)
            s_z = sf[2, a // 4, k] + (rz * to_primal + sign * (ry * to_dual) + z * to_same)
            sf[1, a // 4, k] = s_y
            sf[2, a // 4, k] = s_z
            more = has[a] * fix
            y = y + sign * swap4(own[1, k] * more)
            z = z - sign * swap4(own[0, k] * more)
            ext_y = y * late_primal - sign * (z * late_dual) + swap4(y * late_dual)
            ext_z = z * late_primal + sign * (y * late_dual) + swap4(z * late_dual)
            t_y, t_z = s_y * m_t, s_z * m_t
            ends[a] = (t_y, t_z, ext_y - swap4(t_y), ext_z - swap4(t_z))
        dy = derive_from_ends(ends[0][0], ends[4][0])
        dz = derive_from_ends(ends[0][1], ends[4][1])
        for a in range(5):
            n = 25 * a + k
            got_y, got_z = ci[1, n] - dz[a], ci[2, n] + dy[a]
            if a in ENDS:
                tf[1, a // 4, k] = got_y + ends[a][2]
                tf[2, a // 4, k] = got_z + ends[a][3]
            else:
                final(a, k, ci[0, n], got_y, got_z)
    get = lambda comp, a, k: sf[comp, a // 4, k] * m_t
    yz_into(ENDS, get, tf, lambda a, k: (a // 4, k), cells, final)


def old_plane(sf, si, comp, a, k):
    return sf[comp, a // 4, k] if a in ENDS else si[comp, a - 1, k]


def tree_sum(parts):
    while len(parts) > 1:
        parts = [sum(parts[i : i + 2]) for i in range(0, len(parts), 2)]
    return parts[0]


class Total:
    def __init__(self, zero):
        self.parts, self.turn = [zero] * 8, 0

    def add(self, x):
        self.parts[self.turn] = self.parts[self.turn] + x
        self.turn = (self.turn + 1) % 8

    def value(self):
        return tree_sum(self.parts)


def first_kernel(
    fields, cot, perm_in, reg_in, cond_in, s, sf, lo_ref, hi_ref, aux, tf, perm, reg, cond, sems
):
    row, lane = iotas()
    cells = Cells(row, lane)
    small = [
        pltpu.make_async_copy(src, dst, sems.at[4 + i])
        for i, (src, dst) in enumerate(((perm_in, perm), (reg_in, reg), (cond_in, cond)))
    ]
    copies = [
        pltpu.make_async_copy(src, s.at[:, :, pl.ds(2 * i, 2), :], sems.at[i])
        for i, src in enumerate(
            (fields.at[0:3], cot.at[0:3], fields.at[3:6], cot.at[3:6])
        )
    ]
    for copy in small + copies:
        copy.start()
    for copy in small:
        copy.wait()
    coef, damping = materials(perm, reg, cond, aux)
    for copy in copies:
        copy.wait()
    dual = (row & 2) != 0

    for a in range(5):
        for k in range(25):
            scaled = jnp.where(dual, 1.0 / node_weight(a, k), 1.0)
            for comp in range(3):
                s[comp, 25 * a + k] = s[comp, 25 * a + k] * scaled
    odd_ends(s, sf, tf, lo_ref, hi_ref, row, coef, damping, cells)


def second_kernel(
    sf_in, si, ci, lo_own, hi_own, below, above, aux, layer, cell, node_ref, amp,
    s, sf, lo_ref, hi_ref, g_ref, tf,
):
    row, lane = iotas()
    cells = Cells(row, lane)
    coef, damping = aux[0], aux[1]
    m_t, m_f, m_s = masks(2, row, coef, damping)
    total = Total(jnp.zeros((8, 128), F32))

    def final(a, k, *got):
        for comp in range(3):
            old = old_plane(sf, si, comp, a, k)
            inc = swap4(got[comp]) * m_f + old * m_s
            new = old + inc
            s[comp, 25 * a + k] = new
            total.add(pltpu.roll(inc, 2, 0) * (new * node_weight(a, k)))

    even_half(sf, si, ci, tf, below, above, lo_own, hi_own, row, m_t, cells, final)
    g = total.value()
    node = node_ref[0]
    w = weight_at(node // 25) * weight_at((node // 5) % 5) * weight_at(node % 5)
    incs = source_planes(0, layer, cell, amp, row, lane, coef)
    for comp in range(3):
        new = s[comp, node] + incs[comp]
        s[comp, node] = new
        g = g + pltpu.roll(incs[comp], 2, 0) * (new * w)
    g_ref[...] = g
    odd_ends(s, sf, tf, lo_ref, hi_ref, row, coef, damping, cells)


def third_kernel(
    sf_in, si, ci, lo_own, hi_own, below, above, aux, g_in, layer, cell, node_ref, amp, cot,
    s, g_ref, sf, tf,
):
    row, lane = iotas()
    cells = Cells(row, lane)
    coef, damping = aux[0], aux[1]
    m_t, m_f, m_s = masks(2, row, coef, damping)
    total = Total(jnp.zeros((2, 128), F32))

    def final(a, k, *got):
        for comp in range(3):
            old = old_plane(sf, si, comp, a, k)
            inc = swap4(got[comp]) * m_f + old * m_s
            s[comp, 25 * a + k] = (old + inc) * node_weight(a, k)
            total.add(inc[0:2] * cot[comp, 25 * a + k])

    even_half(sf, si, ci, tf, below, above, lo_own, hi_own, row, m_t, cells, final)
    g = total.value()
    node = node_ref[0]
    incs = source_planes(1, layer, cell, amp, row, lane, coef)
    for comp in range(3):
        g = g + incs[comp][0:2] * cot[comp, node]
    g = g + g_in[2:4]
    g_ref[...] = g * coef[0:2] * (-1.0 / DT)


def store_kernel(s, adj, sems):
    stores = [
        pltpu.make_async_copy(
            s.at[:, :, pl.ds(2 + 4 * i, 2), :], adj.at[3 * i : 3 * i + 3], sems.at[i]
        )
        for i in range(2)
    ]
    for store in stores:
        store.start()
    for store in stores:
        store.wait()


def struct(*shape):
    return jax.ShapeDtypeStruct(shape, F32)


VMEM = pl.BlockSpec(memory_space=pltpu.VMEM)
SMEM = pl.BlockSpec(memory_space=pltpu.SMEM)
HBM = pl.BlockSpec(memory_space=pltpu.HBM)
PARAMS = pltpu.CompilerParams(vmem_limit_bytes=24 * 1024 * 1024)
STATE = (3, 125, 8, 128)
FACES = (3, 2, 25, 8, 128)
INNER = (3, 3, 25, 8, 128)
TRACE = (2, 25, 8, 128)


def exchange(lo, hi):
    peers = lax.axis_size("space")
    up = [(i, (i + 1) % peers) for i in range(peers)]
    down = [((i + 1) % peers, i) for i in range(peers)]
    below = lax.ppermute(hi, "space", up)
    above = lax.ppermute(lo, "space", down)
    return below, above


def src_sum(x):
    for group in ((1, 2, 3), (4, 8, 12)):
        got = [lax.ppermute(x, "src", [(i, i ^ d) for i in range(16)]) for d in group]
        x = (x + got[0]) + (got[1] + got[2])
    return x


def on_device(
    fields, cotangent, permittivity, regions, conductance, src_layer, src_cell, src_node, src_amp
):
    wide = fields.shape[:2] + (2, 128)
    f = fields.reshape(wide)
    cot = cotangent.reshape(wide)
    perm = permittivity.reshape(2, 128)
    reg = regions.reshape(2, 128)
    f, cot, perm, reg, conductance = (
        pltpu.with_memory_space_constraint(x, pltpu.HBM) for x in (f, cot, perm, reg, conductance)
    )
    source = (src_layer, src_cell, src_node, src_amp)
    inner = pl.pallas_call(
        inner_kernel,
        out_shape=(struct(*INNER), struct(*STATE)),
        in_specs=[VMEM] * 2,
        out_specs=[VMEM] * 2,
        compiler_params=PARAMS,
        cost_estimate=pl.CostEstimate(flops=20_000_000, bytes_accessed=1000, transcendentals=0),
        name="inner",
    )
    s, sf, lo, hi, aux = pl.pallas_call(
        first_kernel,
        out_shape=(struct(*STATE), struct(*FACES), struct(*TRACE), struct(*TRACE), struct(2, 8, 128)),
        in_specs=[HBM] * 5,
        out_specs=[VMEM] * 5,
        scratch_shapes=[
            pltpu.VMEM(FACES, F32),
            pltpu.VMEM((2, 128), F32),
            pltpu.VMEM((2, 128), jnp.int32),
            pltpu.SMEM((8,), F32),
            pltpu.SemaphoreType.DMA((7,)),
        ],
        compiler_params=PARAMS,
        name="first",
    )(f, cot, perm, reg, conductance)
    below, above = exchange(lo, hi)
    si, ci = inner(s, aux)
    s, sf, lo, hi, g = pl.pallas_call(
        second_kernel,
        out_shape=(struct(*STATE), struct(*FACES), struct(*TRACE), struct(*TRACE), struct(8, 128)),
        in_specs=[VMEM] * 8 + [SMEM] * 4,
        out_specs=[VMEM] * 5,
        input_output_aliases={0: 1},
        scratch_shapes=[pltpu.VMEM(FACES, F32)],
        compiler_params=PARAMS,
        name="second",
    )(sf, si, ci, lo, hi, below, above, aux, *source)
    below, above = exchange(lo, hi)
    si, ci = inner(s, aux)
    s, g, _ = pl.pallas_call(
        third_kernel,
        out_shape=(struct(*STATE), struct(2, 128), struct(*FACES)),
        in_specs=[VMEM] * 9 + [SMEM] * 4 + [VMEM],
        out_specs=[VMEM] * 3,
        input_output_aliases={0: 2},
        scratch_shapes=[pltpu.VMEM(FACES, F32)],
        compiler_params=PARAMS,
        name="third",
    )(sf, si, ci, lo, hi, below, above, aux, g, *source, cotangent.reshape(wide))
    adjoint = pl.pallas_call(
        store_kernel,
        out_shape=struct(*wide),
        in_specs=[VMEM],
        out_specs=HBM,
        scratch_shapes=[pltpu.SemaphoreType.DMA((2,))],
        compiler_params=PARAMS,
        cost_estimate=pl.CostEstimate(flops=0, bytes_accessed=4_000_000, transcendentals=0),
        name="store",
    )(s)
    gradient = src_sum(g).reshape(permittivity.shape)
    adjoint = with_layout_constraint(adjoint.reshape(fields.shape), Layout((0, 1, 2, 3, 4)))
    return adjoint, gradient


def solution(mesh):
    return jax.shard_map(
        on_device,
        mesh=mesh,
        in_specs=(
            P(None, None, "src", "space", None),
            P(None, None, "src", "space", None),
            P("space", None),
            P("space", None),
            P(),
            P("src"),
            P("src"),
            P("src"),
            P("src", None),
        ),
        out_specs=(P(None, None, "src", "space", None), P("space", None)),
        check_vma=False,
    )
```

time: 65.1 us -> 57 us (0.88)
  local copies, waits for them, and re-layouts: 6.45 us -> 0.01 us
  waiting for transfers between devices: 25.7 us -> 24.3 us
    unnamed x15 -> x4, local copies, waits for them, and re-layouts: 6.02 us -> 0.01 us
    ppermute x2, waiting for transfers between devices: 11.6 us -> 8.97 us  [exchange(): above = lax.ppermute(lo, 'space', down)]
    ppermute x6, waiting for transfers between devices: 2.89 us -> 4.17 us  [src_sum(): lax.ppermute(x, 'src', [(i, i ^ d) for i in range(16)])]
    pallas_call x3 -> x6, Pallas kernels: 10.3 us -> 10 us  [the longest x2 2.65 us: on_device(): si, ci = inner(s, aux)]
  transfers between devices with their start and end apart: 10 -> 10, of which waited for: 7 -> 7; matrix products, arithmetic and copies ran while one was open for 3% -> 0% of each run, Pallas kernels for 0% -> 6%
where the time goes in v2:
time: 57 us; the launch traced here: 56.8 us
  waiting for transfers between devices  24.3 us (43%)
  starting transfers between devices  19.3 us (34%)
  Pallas kernels  10 us (18%)
  between operations  2.64 us (5%)
    ppermute x2, waiting for transfers between devices, exchange(): below = lax.ppermute(hi, 'space', up)  11.1 us
    ppermute x2, starting transfers between devices, exchange(): above = lax.ppermute(lo, 'space', down)  10.3 us
    ppermute x2, waiting for transfers between devices, exchange(): above = lax.ppermute(lo, 'space', down)  8.97 us
    ppermute x6, starting transfers between devices, src_sum(): lax.ppermute(x, 'src', [(i, i ^ d) for i in range(16)])  8.34 us
    ppermute x6, waiting for transfers between devices, src_sum(): lax.ppermute(x, 'src', [(i, i ^ d) for i in range(16)])  4.17 us
    pallas_call x2, Pallas kernels, on_device(): si, ci = inner(s, aux)  2.65 us
    pallas_call x1, Pallas kernels, on_device(): pl.pallas_call(second_kernel, out_shape=(struct(*STATE), struct(*FACES),...  2.52 us
    pallas_call x1, Pallas kernels, on_device(): pl.pallas_call(first_kernel, out_shape=(struct(*STATE), struct(*FACES), s...  2.18 us
  transfers between devices with their start and end apart: 10, of which 7 were waited for; matrix products, arithmetic and copies ran while one was open for 0% of the time, Pallas kernels for 6%

profile of v2, /device:TPU:1, one launch (start us, length us, event | category | flops | bytes accessed | tf_op | source)
XLA Modules:
  0.0 56.8 jit_solution(13375464127413960594)
XLA Ops:
  0.6 0.0 copy-start.1
  0.6 2.2 %first.1 = (f32[3,125,8,128]{3,2,1,0:T(8,128)S(1)}, f32[3,2,25,8,128]{4,3,2,1,0:T(8,128)S(1)}, f32[2,25,8,128]{3,2,1,0:T(8,128)S(1)}, f32[2,25,8,128]{3,2,1,0:T(8,128)S(1)}, f32[2,8,128]{2,1,0:T(8,128)S(1)}) custom-call(f32[6,125,2,128]{3,2,1,0:T(2,128)} %bitcast.8, f32[6,125,2,128]{3,2,1,0:T(2,128)} %bitcast.6, f32[2,128]{1,0:T(2,128)} %bitcast.11, ...), custom_call_target="tpu_custom_call" | custom-call | tf_op jit(solution)/shard_map/first/pallas_call | solution.py:515
  2.8 9.4 %collective-permute-start.1 = (f32[2,25,8,128]{3,2,1,0:T(8,128)S(1)}, f32[2,25,8,128]{3,2,1,0:T(8,128)S(1)}, u32[]{:S(2)}, u32[]{:S(2)}) collective-permute-start(f32[2,25,8,128]{3,2,1,0:T(8,128)S(1)} %get-tuple-element.23.lo_own), channel_id=1, source_target_pairs={{16,0},{32,16},{48,32},{64,48},{80,64},{96,80},{112,96},{128,112},... | collective-permute-start | bytes 614408 | tf_op jit(solution)/shard_map/ppermute | solution.py:483
  12.2 0.0 collective-permute-start
  14.2 1.3 %inner.2 = (f32[3,3,25,8,128]{4,3,2,1,0:T(8,128)S(1)}, f32[3,125,8,128]{3,2,1,0:T(8,128)S(1)}) custom-call(f32[3,125,8,128]{3,2,1,0:T(8,128)S(1)} %get-tuple-element.19.s, f32[2,8,128]{2,1,0:T(8,128)S(1)} %get-tuple-element.20.aux), custom_call_target="tpu_custom_call" | custom-call | flops 20000000 | bytes 1000 | tf_op jit(solution)/shard_map/inner/pallas_call | solution.py:531
  15.5 2.1 %collective-permute-done.1.above = f32[2,25,8,128]{3,2,1,0:T(8,128)S(1)} collective-permute-done((f32[2,25,8,128]{3,2,1,0:T(8,128)S(1)}, f32[2,25,8,128]{3,2,1,0:T(8,128)S(1)}, u32[]{:S(2)}, u32[]{:S(2)}) %collective-permute-start.1) | collective-permute-done | bytes 204832 | tf_op jit(solution)/shard_map/ppermute | solution.py:483
  17.6 8.4 %collective-permute-done.below = f32[2,25,8,128]{3,2,1,0:T(8,128)S(1)} collective-permute-done((f32[2,25,8,128]{3,2,1,0:T(8,128)S(1)}, f32[2,25,8,128]{3,2,1,0:T(8,128)S(1)}, u32[]{:S(2)}, u32[]{:S(2)}) %collective-permute-start) | collective-permute-done | bytes 204832 | tf_op jit(solution)/shard_map/ppermute | solution.py:482
  26.0 0.0 copy-done.1
  26.0 2.5 %second.1 = (f32[3,125,8,128]{3,2,1,0:T(8,128)S(1)}, f32[3,2,25,8,128]{4,3,2,1,0:T(8,128)S(1)}, f32[2,25,8,128]{3,2,1,0:T(8,128)S(1)}, f32[2,25,8,128]{3,2,1,0:T(8,128)S(1)}, f32[8,128]{1,0:T(8,128)S(1)}) custom-call(f32[3,2,25,8,128]{4,3,2,1,0:T(8,128)S(1)} %get-tuple-element.18.sf_in, ...), custom_call_target="tpu_custom_call", output_to_operand_aliasing={{1}: (0, {})} | custom-call | tf_op jit(solution)/shard_map/second/pallas_call | solution.py:532
  28.5 0.0 copy-start
  28.5 0.9 %collective-permute-start.3 = (f32[2,25,8,128]{3,2,1,0:T(8,128)S(1)}, f32[2,25,8,128]{3,2,1,0:T(8,128)S(1)}, u32[]{:S(2)}, u32[]{:S(2)}) collective-permute-start(f32[2,25,8,128]{3,2,1,0:T(8,128)S(1)} %get-tuple-element.29.lo_own), channel_id=1, source_target_pairs={{16,0},{32,16},{48,32},{64,48},{80,64},{96,80},{112,96},{128,112},... | collective-permute-start | bytes 614408 | tf_op jit(solution)/shard_map/ppermute | solution.py:483
  29.4 0.6 %collective-permute-start.2 = (f32[2,25,8,128]{3,2,1,0:T(8,128)S(1)}, f32[2,25,8,128]{3,2,1,0:T(8,128)S(1)}, u32[]{:S(2)}, u32[]{:S(2)}) collective-permute-start(f32[2,25,8,128]{3,2,1,0:T(8,128)S(1)} %get-tuple-element.30.hi_own), channel_id=1, source_target_pairs={{0,16},{16,32},{32,48},{48,64},{64,80},{80,96},{96,112},{112,128},... | collective-permute-start | bytes 614408 | tf_op jit(solution)/shard_map/ppermute | solution.py:482
  30.1 1.3 %inner.3 = (f32[3,3,25,8,128]{4,3,2,1,0:T(8,128)S(1)}, f32[3,125,8,128]{3,2,1,0:T(8,128)S(1)}) custom-call(f32[3,125,8,128]{3,2,1,0:T(8,128)S(1)} %get-tuple-element.26.s, f32[2,8,128]{2,1,0:T(8,128)S(1)} %get-tuple-element.20.aux), custom_call_target="tpu_custom_call" | custom-call | flops 20000000 | bytes 1000 | tf_op jit(solution)/shard_map/inner/pallas_call | solution.py:543
  31.4 6.8 %collective-permute-done.3.above = f32[2,25,8,128]{3,2,1,0:T(8,128)S(1)} collective-permute-done((f32[2,25,8,128]{3,2,1,0:T(8,128)S(1)}, f32[2,25,8,128]{3,2,1,0:T(8,128)S(1)}, u32[]{:S(2)}, u32[]{:S(2)}) %collective-permute-start.3) | collective-permute-done | bytes 204832 | tf_op jit(solution)/shard_map/ppermute | solution.py:483
  38.3 2.7 %collective-permute-done.2.below = f32[2,25,8,128]{3,2,1,0:T(8,128)S(1)} collective-permute-done((f32[2,25,8,128]{3,2,1,0:T(8,128)S(1)}, f32[2,25,8,128]{3,2,1,0:T(8,128)S(1)}, u32[]{:S(2)}, u32[]{:S(2)}) %collective-permute-start.2) | collective-permute-done | bytes 204832 | tf_op jit(solution)/shard_map/ppermute | solution.py:482
  41.0 0.0 copy-done
  41.0 1.8 %third.1 = (f32[3,125,8,128]{3,2,1,0:T(8,128)S(1)}, f32[2,128]{1,0:T(2,128)S(1)}, f32[3,2,25,8,128]{4,3,2,1,0:T(8,128)S(1)}) custom-call(f32[3,2,25,8,128]{4,3,2,1,0:T(8,128)S(1)} %get-tuple-element.25.sf_in, f32[3,3,25,8,128]{4,3,2,1,0:T(8,128)S(1)} %get-tuple-element.27.si, ...), custom_call_target="tpu_custom_call", output_to_operand_aliasing={{2}: (0, {})} | custom-call | tf_op jit(solution)/shard_map/third/pallas_call | solution.py:544
  42.8 4.5 %collective-permute-start.6 = (f32[2,128]{1,0:T(2,128)S(1)}, f32[2,128]{1,0:T(2,128)S(1)}, u32[]{:S(2)}, u32[]{:S(2)}) collective-permute-start(f32[2,128]{1,0:T(2,128)S(1)} %get-tuple-element.33), channel_id=1, source_target_pairs={{0,3},{1,2},{2,1},{3,0},{4,7},{5,6},{6,5},{7,4},{8,11},{9,10},{10,... | collective-permute-start | bytes 3080 | tf_op jit(solution)/shard_map/ppermute | solution.py:489
  47.3 0.0 collective-permute-start.5
  47.3 0.5 collective-permute-start.4
  47.8 0.8 %collective-permute-done.6 = f32[2,128]{1,0:T(2,128)S(1)} collective-permute-done((f32[2,128]{1,0:T(2,128)S(1)}, f32[2,128]{1,0:T(2,128)S(1)}, u32[]{:S(2)}, u32[]{:S(2)}) %collective-permute-start.6) | collective-permute-done | bytes 1056 | tf_op jit(solution)/shard_map/ppermute | solution.py:489
  48.6 1.2 %collective-permute-done.5 = f32[2,128]{1,0:T(2,128)S(1)} collective-permute-done((f32[2,128]{1,0:T(2,128)S(1)}, f32[2,128]{1,0:T(2,128)S(1)}, u32[]{:S(2)}, u32[]{:S(2)}) %collective-permute-start.5) | collective-permute-done | bytes 1056 | tf_op jit(solution)/shard_map/ppermute | solution.py:489
  49.8 0.0 collective-permute-done.4
  49.8 2.6 %collective-permute-start.9 = (f32[2,128]{1,0:T(2,128)S(1)}, f32[2,128]{1,0:T(2,128)S(1)}, u32[]{:S(2)}, u32[]{:S(2)}) collective-permute-start(f32[2,128]{1,0:T(2,128)S(1)} %add_add_fusion.1), channel_id=1, source_target_pairs={{0,12},{1,13},{2,14},{3,15},{4,8},{5,9},{6,10},{7,11},{8,4},{9,5},... | collective-permute-start | bytes 3080 | tf_op jit(solution)/shard_map/ppermute | solution.py:489
  52.3 0.5 collective-permute-start.8
  52.8 0.3 collective-permute-start.7
  53.1 0.9 %store.1 = f32[6,125,2,128]{3,2,1,0:T(2,128)} custom-call(f32[3,125,8,128]{3,2,1,0:T(8,128)S(1)} %get-tuple-element.32.s), custom_call_target="tpu_custom_call" | custom-call | bytes 4000000 | tf_op jit(solution)/shard_map/store/pallas_call | solution.py:554
  54.0 0.0 collective-permute-done.9
  54.0 2.2 %collective-permute-done.8 = f32[2,128]{1,0:T(2,128)S(1)} collective-permute-done((f32[2,128]{1,0:T(2,128)S(1)}, f32[2,128]{1,0:T(2,128)S(1)}, u32[]{:S(2)}, u32[]{:S(2)}) %collective-permute-start.8) | collective-permute-done | bytes 1056 | tf_op jit(solution)/shard_map/ppermute | solution.py:489
  56.3 0.0 collective-permute-done.7
  56.3 0.6 add_add_fusion
  (1 shorter events, 0.0 us)
Async XLA Ops:
  0.6 25.4 %copy-start.1 = (f32[1,6]{1,0:T(1,128)S(1)}, f32[1,6]{1,0:T(1,128)}, u32[]{:S(2)}) copy-start(f32[1,6]{1,0:T(1,128)} %amp.3) | copy-start | bytes 76
  2.8 14.8 %collective-permute-start.1 = (f32[2,25,8,128]{3,2,1,0:T(8,128)S(1)}, f32[2,25,8,128]{3,2,1,0:T(8,128)S(1)}, u32[]{:S(2)}, u32[]{:S(2)}) collective-permute-start(f32[2,25,8,128]{3,2,1,0:T(8,128)S(1)} %get-tuple-element.23.lo_own), channel_id=1, source_target_pairs={{16,0},{32,16},{48,32},{64,48},{80,64},{96,80},{112,96},{128,112},... | collective-permute-start | bytes 614408 | tf_op jit(solution)/shard_map/ppermute | solution.py:483
  12.2 13.8 %collective-permute-start = (f32[2,25,8,128]{3,2,1,0:T(8,128)S(1)}, f32[2,25,8,128]{3,2,1,0:T(8,128)S(1)}, u32[]{:S(2)}, u32[]{:S(2)}) collective-permute-start(f32[2,25,8,128]{3,2,1,0:T(8,128)S(1)} %get-tuple-element.24.hi_own), channel_id=1, source_target_pairs={{0,16},{16,32},{32,48},{48,64},{64,80},{80,96},{96,112},{112,128},... | collective-permute-start | bytes 614408 | tf_op jit(solution)/shard_map/ppermute | solution.py:482
  28.5 12.5 %copy-start = (f32[6,125,1,1,256]{4,3,2,1,0:T(1,128)S(1)}, f32[6,125,1,1,256]{4,3,2,1,0:T(1,128)}, u32[]{:S(2)}) copy-start(f32[6,125,1,1,256]{4,3,2,1,0:T(1,128)} %param.10) | copy-start | bytes 2304004
  28.5 9.7 %collective-permute-start.3 = (f32[2,25,8,128]{3,2,1,0:T(8,128)S(1)}, f32[2,25,8,128]{3,2,1,0:T(8,128)S(1)}, u32[]{:S(2)}, u32[]{:S(2)}) collective-permute-start(f32[2,25,8,128]{3,2,1,0:T(8,128)S(1)} %get-tuple-element.29.lo_own), channel_id=1, source_target_pairs={{16,0},{32,16},{48,32},{64,48},{80,64},{96,80},{112,96},{128,112},... | collective-permute-start | bytes 614408 | tf_op jit(solution)/shard_map/ppermute | solution.py:483
  29.4 11.6 %collective-permute-start.2 = (f32[2,25,8,128]{3,2,1,0:T(8,128)S(1)}, f32[2,25,8,128]{3,2,1,0:T(8,128)S(1)}, u32[]{:S(2)}, u32[]{:S(2)}) collective-permute-start(f32[2,25,8,128]{3,2,1,0:T(8,128)S(1)} %get-tuple-element.30.hi_own), channel_id=1, source_target_pairs={{0,16},{16,32},{32,48},{48,64},{64,80},{80,96},{96,112},{112,128},... | collective-permute-start | bytes 614408 | tf_op jit(solution)/shard_map/ppermute | solution.py:482
  42.8 5.8 %collective-permute-start.6 = (f32[2,128]{1,0:T(2,128)S(1)}, f32[2,128]{1,0:T(2,128)S(1)}, u32[]{:S(2)}, u32[]{:S(2)}) collective-permute-start(f32[2,128]{1,0:T(2,128)S(1)} %get-tuple-element.33), channel_id=1, source_target_pairs={{0,3},{1,2},{2,1},{3,0},{4,7},{5,6},{6,5},{7,4},{8,11},{9,10},{10,... | collective-permute-start | bytes 3080 | tf_op jit(solution)/shard_map/ppermute | solution.py:489
  47.3 2.4 %collective-permute-start.5 = (f32[2,128]{1,0:T(2,128)S(1)}, f32[2,128]{1,0:T(2,128)S(1)}, u32[]{:S(2)}, u32[]{:S(2)}) collective-permute-start(f32[2,128]{1,0:T(2,128)S(1)} %get-tuple-element.33), channel_id=1, source_target_pairs={{0,2},{1,3},{2,0},{3,1},{4,6},{5,7},{6,4},{7,5},{8,10},{9,11},{10,... | collective-permute-start | bytes 3080 | tf_op jit(solution)/shard_map/ppermute | solution.py:489
  47.3 2.4 %collective-permute-start.4 = (f32[2,128]{1,0:T(2,128)S(1)}, f32[2,128]{1,0:T(2,128)S(1)}, u32[]{:S(2)}, u32[]{:S(2)}) collective-permute-start(f32[2,128]{1,0:T(2,128)S(1)} %get-tuple-element.33), channel_id=1, source_target_pairs={{0,1},{1,0},{2,3},{3,2},{4,5},{5,4},{6,7},{7,6},{8,9},{9,8},{10,11... | collective-permute-start | bytes 3080 | tf_op jit(solution)/shard_map/ppermute | solution.py:489
  49.8 4.2 %collective-permute-start.9 = (f32[2,128]{1,0:T(2,128)S(1)}, f32[2,128]{1,0:T(2,128)S(1)}, u32[]{:S(2)}, u32[]{:S(2)}) collective-permute-start(f32[2,128]{1,0:T(2,128)S(1)} %add_add_fusion.1), channel_id=1, source_target_pairs={{0,12},{1,13},{2,14},{3,15},{4,8},{5,9},{6,10},{7,11},{8,4},{9,5},... | collective-permute-start | bytes 3080 | tf_op jit(solution)/shard_map/ppermute | solution.py:489
  52.3 3.9 %collective-permute-start.8 = (f32[2,128]{1,0:T(2,128)S(1)}, f32[2,128]{1,0:T(2,128)S(1)}, u32[]{:S(2)}, u32[]{:S(2)}) collective-permute-start(f32[2,128]{1,0:T(2,128)S(1)} %add_add_fusion.1), channel_id=1, source_target_pairs={{0,8},{1,9},{2,10},{3,11},{4,12},{5,13},{6,14},{7,15},{8,0},{9,1},... | collective-permute-start | bytes 3080 | tf_op jit(solution)/shard_map/ppermute | solution.py:489
  52.8 3.4 %collective-permute-start.7 = (f32[2,128]{1,0:T(2,128)S(1)}, f32[2,128]{1,0:T(2,128)S(1)}, u32[]{:S(2)}, u32[]{:S(2)}) collective-permute-start(f32[2,128]{1,0:T(2,128)S(1)} %add_add_fusion.1), channel_id=1, source_target_pairs={{0,4},{1,5},{2,6},{3,7},{4,0},{5,1},{6,2},{7,3},{8,12},{9,13},{10,... | collective-permute-start | bytes 3080 | tf_op jit(solution)/shard_map/ppermute | solution.py:489

commit v3 on v2

--- a/solution.py
+++ b/solution.py
@@ -477,11 +477,13 @@
 
 def exchange(lo, hi):
     peers = lax.axis_size("space")
-    up = [(i, (i + 1) % peers) for i in range(peers)]
-    down = [((i + 1) % peers, i) for i in range(peers)]
-    below = lax.ppermute(hi, "space", up)
-    above = lax.ppermute(lo, "space", down)
-    return below, above
+    even = lax.axis_index("space") % 2 == 0
+    inner_pairs = [(i, i ^ 1) for i in range(peers)]
+    outer_pairs = [(i, (i + 2 * (i % 2) - 1) % peers) for i in range(peers)]
+    one, two = lax.optimization_barrier((jnp.where(even, lo, hi), jnp.where(even, hi, lo)))
+    got_one = lax.ppermute(one, "space", outer_pairs)
+    got_two = lax.ppermute(two, "space", inner_pairs)
+    return jnp.where(even, got_one, got_two), jnp.where(even, got_two, got_one)
 
 
 def src_sum(x):

time: 57 us -> 51.8 us (0.909)
  waiting for transfers between devices: 24.3 us -> 13.3 us
  starting transfers between devices: 19.3 us -> 24.9 us
    ppermute x4, waiting for transfers between devices: 20.1 us -> 9.82 us  [the longest x2 9.81 us: exchange(): got_one = lax.ppermute(one, 'space', outer_pairs)]
    ppermute x4, starting transfers between devices: 10.9 us -> 18.1 us  [the longest x2 18.1 us: exchange(): got_one = lax.ppermute(one, 'space', outer_pairs)]
    ppermute x6, starting transfers between devices: 8.34 us -> 6.77 us  [src_sum(): lax.ppermute(x, 'src', [(i, i ^ d) for i in range(16)])]
    ppermute x6, waiting for transfers between devices: 4.17 us -> 3.49 us  [src_sum(): lax.ppermute(x, 'src', [(i, i ^ d) for i in range(16)])]
  transfers between devices with their start and end apart: 10 -> 10, of which waited for: 7 -> 4; matrix products, arithmetic and copies ran while one was open for 0% -> 0% of each run, Pallas kernels for 6% -> 7%
where the time goes in v3:
time: 51.8 us; the launch traced here: 51.7 us
  starting transfers between devices  24.9 us (48%)
  waiting for transfers between devices  13.3 us (26%)
  Pallas kernels  10 us (19%)
  between operations  2.68 us (5%)
  other arithmetic  0.72 us (1%)
    ppermute x2, starting transfers between devices, exchange(): got_one = lax.ppermute(one, 'space', outer_pairs)  18.1 us
    ppermute x2, waiting for transfers between devices, exchange(): got_one = lax.ppermute(one, 'space', outer_pairs)  9.81 us
    ppermute x6, starting transfers between devices, src_sum(): lax.ppermute(x, 'src', [(i, i ^ d) for i in range(16)])  6.77 us
    ppermute x6, waiting for transfers between devices, src_sum(): lax.ppermute(x, 'src', [(i, i ^ d) for i in range(16)])  3.49 us
    pallas_call x2, Pallas kernels, on_device(): si, ci = inner(s, aux)  2.65 us
    pallas_call x1, Pallas kernels, on_device(): pl.pallas_call(second_kernel, out_shape=(struct(*STATE), struct(*FACES),...  2.52 us
    pallas_call x1, Pallas kernels, on_device(): pl.pallas_call(first_kernel, out_shape=(struct(*STATE), struct(*FACES), s...  2.18 us
    pallas_call x1, Pallas kernels, on_device(): pl.pallas_call(third_kernel, out_shape=(struct(*STATE), struct(2, 128), s...  1.81 us
  transfers between devices with their start and end apart: 10, of which 4 were waited for; matrix products, arithmetic and copies ran while one was open for 0% of the time, Pallas kernels for 7%

profile of v3, /device:TPU:1, one launch (start us, length us, event | category | flops | bytes accessed | tf_op | source)
XLA Modules:
  0.0 51.7 jit_solution(4693611012385960792)
XLA Ops:
  0.6 2.2 %first.1 = (f32[3,125,8,128]{3,2,1,0:T(8,128)S(1)}, f32[3,2,25,8,128]{4,3,2,1,0:T(8,128)S(1)}, f32[2,25,8,128]{3,2,1,0:T(8,128)S(1)}, f32[2,25,8,128]{3,2,1,0:T(8,128)S(1)}, f32[2,8,128]{2,1,0:T(8,128)S(1)}) custom-call(f32[6,125,2,128]{3,2,1,0:T(2,128)} %bitcast.8, f32[6,125,2,128]{3,2,1,0:T(2,128)} %bitcast.6, f32[2,128]{1,0:T(2,128)} %bitcast.11, ...), custom_call_target="tpu_custom_call" | custom-call | tf_op jit(solution)/shard_map/first/pallas_call | solution.py:517
  2.8 0.0 copy-start.1
  2.9 9.4 %collective-permute-start = (f32[2,25,8,128]{3,2,1,0:T(8,128)S(1)}, f32[2,25,8,128]{3,2,1,0:T(8,128)S(1)}, u32[]{:S(2)}, u32[]{:S(2)}) collective-permute-start(f32[2,25,8,128]{3,2,1,0:T(8,128)S(1)} %get-tuple-element.29), channel_id=1, source_target_pairs={{0,240},{16,32},{32,16},{48,64},{64,48},{80,96},{96,80},{112,128},... | collective-permute-start | bytes 614408 | tf_op jit(solution)/shard_map/ppermute | solution.py:484
  12.3 0.0 collective-permute-start.1
  14.2 1.3 %inner.2 = (f32[3,3,25,8,128]{4,3,2,1,0:T(8,128)S(1)}, f32[3,125,8,128]{3,2,1,0:T(8,128)S(1)}) custom-call(f32[3,125,8,128]{3,2,1,0:T(8,128)S(1)} %get-tuple-element.23.s, f32[2,8,128]{2,1,0:T(8,128)S(1)} %get-tuple-element.24.aux), custom_call_target="tpu_custom_call" | custom-call | flops 20000000 | bytes 1000 | tf_op jit(solution)/shard_map/inner/pallas_call | solution.py:533
  15.5 2.7 %collective-permute-done = f32[2,25,8,128]{3,2,1,0:T(8,128)S(1)} collective-permute-done((f32[2,25,8,128]{3,2,1,0:T(8,128)S(1)}, f32[2,25,8,128]{3,2,1,0:T(8,128)S(1)}, u32[]{:S(2)}, u32[]{:S(2)}) %collective-permute-start) | collective-permute-done | bytes 204832 | tf_op jit(solution)/shard_map/ppermute | solution.py:484
  18.3 0.0 collective-permute-done.1
  18.3 0.0 copy-done.1
  18.3 2.5 %second.1 = (f32[3,125,8,128]{3,2,1,0:T(8,128)S(1)}, f32[3,2,25,8,128]{4,3,2,1,0:T(8,128)S(1)}, f32[2,25,8,128]{3,2,1,0:T(8,128)S(1)}, f32[2,25,8,128]{3,2,1,0:T(8,128)S(1)}, f32[8,128]{1,0:T(8,128)S(1)}) custom-call(f32[3,2,25,8,128]{4,3,2,1,0:T(8,128)S(1)} %get-tuple-element.22.sf_in, ...), custom_call_target="tpu_custom_call", output_to_operand_aliasing={{1}: (0, {})} | custom-call | tf_op jit(solution)/shard_map/second/pallas_call | solution.py:534
  20.8 0.0 copy-start
  20.9 8.7 %collective-permute-start.2 = (f32[2,25,8,128]{3,2,1,0:T(8,128)S(1)}, f32[2,25,8,128]{3,2,1,0:T(8,128)S(1)}, u32[]{:S(2)}, u32[]{:S(2)}) collective-permute-start(f32[2,25,8,128]{3,2,1,0:T(8,128)S(1)} %get-tuple-element.37), channel_id=1, source_target_pairs={{0,240},{16,32},{32,16},{48,64},{64,48},{80,96},{96,80},{112,128},... | collective-permute-start | bytes 614408 | tf_op jit(solution)/shard_map/ppermute | solution.py:484
  29.6 0.0 collective-permute-start.3
  29.6 1.3 %inner.3 = (f32[3,3,25,8,128]{4,3,2,1,0:T(8,128)S(1)}, f32[3,125,8,128]{3,2,1,0:T(8,128)S(1)}) custom-call(f32[3,125,8,128]{3,2,1,0:T(8,128)S(1)} %get-tuple-element.32.s, f32[2,8,128]{2,1,0:T(8,128)S(1)} %get-tuple-element.24.aux), custom_call_target="tpu_custom_call" | custom-call | flops 20000000 | bytes 1000 | tf_op jit(solution)/shard_map/inner/pallas_call | solution.py:545
  31.0 7.1 %collective-permute-done.2 = f32[2,25,8,128]{3,2,1,0:T(8,128)S(1)} collective-permute-done((f32[2,25,8,128]{3,2,1,0:T(8,128)S(1)}, f32[2,25,8,128]{3,2,1,0:T(8,128)S(1)}, u32[]{:S(2)}, u32[]{:S(2)}) %collective-permute-start.2) | collective-permute-done | bytes 204832 | tf_op jit(solution)/shard_map/ppermute | solution.py:484
  38.1 0.0 collective-permute-done.3
  38.1 0.0 copy-done
  38.1 1.8 %third.1 = (f32[3,125,8,128]{3,2,1,0:T(8,128)S(1)}, f32[2,128]{1,0:T(2,128)S(1)}, f32[3,2,25,8,128]{4,3,2,1,0:T(8,128)S(1)}) custom-call(f32[3,2,25,8,128]{4,3,2,1,0:T(8,128)S(1)} %get-tuple-element.31.sf_in, f32[3,3,25,8,128]{4,3,2,1,0:T(8,128)S(1)} %get-tuple-element.33.si, ...), custom_call_target="tpu_custom_call", output_to_operand_aliasing={{2}: (0, {})} | custom-call | tf_op jit(solution)/shard_map/third/pallas_call | solution.py:546
  39.9 0.8 %collective-permute-start.6 = (f32[2,128]{1,0:T(2,128)S(1)}, f32[2,128]{1,0:T(2,128)S(1)}, u32[]{:S(2)}, u32[]{:S(2)}) collective-permute-start(f32[2,128]{1,0:T(2,128)S(1)} %get-tuple-element.41), channel_id=1, source_target_pairs={{0,3},{1,2},{2,1},{3,0},{4,7},{5,6},{6,5},{7,4},{8,11},{9,10},{10,... | collective-permute-start | bytes 3080 | tf_op jit(solution)/shard_map/ppermute | solution.py:491
  40.7 2.7 %collective-permute-start.5 = (f32[2,128]{1,0:T(2,128)S(1)}, f32[2,128]{1,0:T(2,128)S(1)}, u32[]{:S(2)}, u32[]{:S(2)}) collective-permute-start(f32[2,128]{1,0:T(2,128)S(1)} %get-tuple-element.41), channel_id=1, source_target_pairs={{0,2},{1,3},{2,0},{3,1},{4,6},{5,7},{6,4},{7,5},{8,10},{9,11},{10,... | collective-permute-start | bytes 3080 | tf_op jit(solution)/shard_map/ppermute | solution.py:491
  43.3 0.0 collective-permute-start.4
  43.3 0.0 collective-permute-done.6
  43.3 1.2 %collective-permute-done.5 = f32[2,128]{1,0:T(2,128)S(1)} collective-permute-done((f32[2,128]{1,0:T(2,128)S(1)}, f32[2,128]{1,0:T(2,128)S(1)}, u32[]{:S(2)}, u32[]{:S(2)}) %collective-permute-start.5) | collective-permute-done | bytes 1056 | tf_op jit(solution)/shard_map/ppermute | solution.py:491
  44.6 0.0 collective-permute-done.4
  44.6 2.6 %collective-permute-start.9 = (f32[2,128]{1,0:T(2,128)S(1)}, f32[2,128]{1,0:T(2,128)S(1)}, u32[]{:S(2)}, u32[]{:S(2)}) collective-permute-start(f32[2,128]{1,0:T(2,128)S(1)} %add_add_fusion.1), channel_id=1, source_target_pairs={{0,12},{1,13},{2,14},{3,15},{4,8},{5,9},{6,10},{7,11},{8,4},{9,5},... | collective-permute-start | bytes 3080 | tf_op jit(solution)/shard_map/ppermute | solution.py:491
  47.2 0.5 %collective-permute-start.8 = (f32[2,128]{1,0:T(2,128)S(1)}, f32[2,128]{1,0:T(2,128)S(1)}, u32[]{:S(2)}, u32[]{:S(2)}) collective-permute-start(f32[2,128]{1,0:T(2,128)S(1)} %add_add_fusion.1), channel_id=1, source_target_pairs={{0,8},{1,9},{2,10},{3,11},{4,12},{5,13},{6,14},{7,15},{8,0},{9,1},... | collective-permute-start | bytes 3080 | tf_op jit(solution)/shard_map/ppermute | solution.py:491
  47.7 0.3 collective-permute-start.7
  47.9 0.9 %store.1 = f32[6,125,2,128]{3,2,1,0:T(2,128)} custom-call(f32[3,125,8,128]{3,2,1,0:T(8,128)S(1)} %get-tuple-element.40.s), custom_call_target="tpu_custom_call" | custom-call | bytes 4000000 | tf_op jit(solution)/shard_map/store/pallas_call | solution.py:556
  48.8 0.0 collective-permute-done.9
  48.8 2.2 %collective-permute-done.8 = f32[2,128]{1,0:T(2,128)S(1)} collective-permute-done((f32[2,128]{1,0:T(2,128)S(1)}, f32[2,128]{1,0:T(2,128)S(1)}, u32[]{:S(2)}, u32[]{:S(2)}) %collective-permute-start.8) | collective-permute-done | bytes 1056 | tf_op jit(solution)/shard_map/ppermute | solution.py:491
  51.1 0.0 collective-permute-done.7
  51.1 0.6 %add_add_fusion = f32[2,128]{1,0:T(2,128)} fusion(f32[2,128]{1,0:T(2,128)S(1)} %collective-permute-done.8, f32[2,128]{1,0:T(2,128)S(1)} %collective-permute-done.9, f32[2,128]{1,0:T(2,128)S(1)} %add_add_fusion.1, f32[2,128]{1,0:T(2,128)S(1)} %collective-permute-done.7), kind=kLoop, calls=%fused_computation.8 | loop fusion | flops 768 | bytes 5120 | tf_op jit(solution)/shard_map/add | solution.py:492
  (5 shorter events, 0.2 us)
Async XLA Ops:
  2.8 15.5 %copy-start.1 = (f32[1,6]{1,0:T(1,128)S(1)}, f32[1,6]{1,0:T(1,128)}, u32[]{:S(2)}) copy-start(f32[1,6]{1,0:T(1,128)} %amp.3) | copy-start | bytes 76
  2.9 15.4 %collective-permute-start = (f32[2,25,8,128]{3,2,1,0:T(8,128)S(1)}, f32[2,25,8,128]{3,2,1,0:T(8,128)S(1)}, u32[]{:S(2)}, u32[]{:S(2)}) collective-permute-start(f32[2,25,8,128]{3,2,1,0:T(8,128)S(1)} %get-tuple-element.29), channel_id=1, source_target_pairs={{0,240},{16,32},{32,16},{48,64},{64,48},{80,96},{96,80},{112,128},... | collective-permute-start | bytes 614408 | tf_op jit(solution)/shard_map/ppermute | solution.py:484
  12.3 6.0 %collective-permute-start.1 = (f32[2,25,8,128]{3,2,1,0:T(8,128)S(1)}, f32[2,25,8,128]{3,2,1,0:T(8,128)S(1)}, u32[]{:S(2)}, u32[]{:S(2)}) collective-permute-start(f32[2,25,8,128]{3,2,1,0:T(8,128)S(1)} %get-tuple-element.30), channel_id=1, source_target_pairs={{0,16},{16,0},{32,48},{48,32},{64,80},{80,64},{96,112},{112,96},{1... | collective-permute-start | bytes 614408 | tf_op jit(solution)/shard_map/ppermute | solution.py:485
  20.8 17.2 %copy-start = (f32[6,125,1,1,256]{4,3,2,1,0:T(1,128)S(1)}, f32[6,125,1,1,256]{4,3,2,1,0:T(1,128)}, u32[]{:S(2)}) copy-start(f32[6,125,1,1,256]{4,3,2,1,0:T(1,128)} %param.10) | copy-start | bytes 2304004
  20.9 17.2 %collective-permute-start.2 = (f32[2,25,8,128]{3,2,1,0:T(8,128)S(1)}, f32[2,25,8,128]{3,2,1,0:T(8,128)S(1)}, u32[]{:S(2)}, u32[]{:S(2)}) collective-permute-start(f32[2,25,8,128]{3,2,1,0:T(8,128)S(1)} %get-tuple-element.37), channel_id=1, source_target_pairs={{0,240},{16,32},{32,16},{48,64},{64,48},{80,96},{96,80},{112,128},... | collective-permute-start | bytes 614408 | tf_op jit(solution)/shard_map/ppermute | solution.py:484
  29.6 8.4 %collective-permute-start.3 = (f32[2,25,8,128]{3,2,1,0:T(8,128)S(1)}, f32[2,25,8,128]{3,2,1,0:T(8,128)S(1)}, u32[]{:S(2)}, u32[]{:S(2)}) collective-permute-start(f32[2,25,8,128]{3,2,1,0:T(8,128)S(1)} %get-tuple-element.38), channel_id=1, source_target_pairs={{0,16},{16,0},{32,48},{48,32},{64,80},{80,64},{96,112},{112,96},{1... | collective-permute-start | bytes 614408 | tf_op jit(solution)/shard_map/ppermute | solution.py:485
  39.9 3.4 %collective-permute-start.6 = (f32[2,128]{1,0:T(2,128)S(1)}, f32[2,128]{1,0:T(2,128)S(1)}, u32[]{:S(2)}, u32[]{:S(2)}) collective-permute-start(f32[2,128]{1,0:T(2,128)S(1)} %get-tuple-element.41), channel_id=1, source_target_pairs={{0,3},{1,2},{2,1},{3,0},{4,7},{5,6},{6,5},{7,4},{8,11},{9,10},{10,... | collective-permute-start | bytes 3080 | tf_op jit(solution)/shard_map/ppermute | solution.py:491
  40.7 3.9 %collective-permute-start.5 = (f32[2,128]{1,0:T(2,128)S(1)}, f32[2,128]{1,0:T(2,128)S(1)}, u32[]{:S(2)}, u32[]{:S(2)}) collective-permute-start(f32[2,128]{1,0:T(2,128)S(1)} %get-tuple-element.41), channel_id=1, source_target_pairs={{0,2},{1,3},{2,0},{3,1},{4,6},{5,7},{6,4},{7,5},{8,10},{9,11},{10,... | collective-permute-start | bytes 3080 | tf_op jit(solution)/shard_map/ppermute | solution.py:491
  43.3 1.3 %collective-permute-start.4 = (f32[2,128]{1,0:T(2,128)S(1)}, f32[2,128]{1,0:T(2,128)S(1)}, u32[]{:S(2)}, u32[]{:S(2)}) collective-permute-start(f32[2,128]{1,0:T(2,128)S(1)} %get-tuple-element.41), channel_id=1, source_target_pairs={{0,1},{1,0},{2,3},{3,2},{4,5},{5,4},{6,7},{7,6},{8,9},{9,8},{10,11... | collective-permute-start | bytes 3080 | tf_op jit(solution)/shard_map/ppermute | solution.py:491
  44.6 4.2 %collective-permute-start.9 = (f32[2,128]{1,0:T(2,128)S(1)}, f32[2,128]{1,0:T(2,128)S(1)}, u32[]{:S(2)}, u32[]{:S(2)}) collective-permute-start(f32[2,128]{1,0:T(2,128)S(1)} %add_add_fusion.1), channel_id=1, source_target_pairs={{0,12},{1,13},{2,14},{3,15},{4,8},{5,9},{6,10},{7,11},{8,4},{9,5},... | collective-permute-start | bytes 3080 | tf_op jit(solution)/shard_map/ppermute | solution.py:491
  47.2 3.9 %collective-permute-start.8 = (f32[2,128]{1,0:T(2,128)S(1)}, f32[2,128]{1,0:T(2,128)S(1)}, u32[]{:S(2)}, u32[]{:S(2)}) collective-permute-start(f32[2,128]{1,0:T(2,128)S(1)} %add_add_fusion.1), channel_id=1, source_target_pairs={{0,8},{1,9},{2,10},{3,11},{4,12},{5,13},{6,14},{7,15},{8,0},{9,1},... | collective-permute-start | bytes 3080 | tf_op jit(solution)/shard_map/ppermute | solution.py:491
  47.7 3.4 %collective-permute-start.7 = (f32[2,128]{1,0:T(2,128)S(1)}, f32[2,128]{1,0:T(2,128)S(1)}, u32[]{:S(2)}, u32[]{:S(2)}) collective-permute-start(f32[2,128]{1,0:T(2,128)S(1)} %add_add_fusion.1), channel_id=1, source_target_pairs={{0,4},{1,5},{2,6},{3,7},{4,0},{5,1},{6,2},{7,3},{8,12},{9,13},{10,... | collective-permute-start | bytes 3080 | tf_op jit(solution)/shard_map/ppermute | solution.py:491

commit v4 on v3

--- a/solution.py
+++ b/solution.py
@@ -309,7 +309,7 @@
     for k in range(25):
         ends = {}
         for a, sign, got, own in ((0, -1.0, below, lo_own), (4, 1.0, above, hi_own)):
-            y, z = got[0, k] * has[a], got[1, k] * has[a]
+            y, z = got(0, k) * has[a], got(1, k) * has[a]
             ry, rz = swap4(y), swap4(z)
             s_y = sf[1, a // 4, k] + (ry * to_primal - sign * (rz * to_dual) + y * to_same)
             s_z = sf[2, a // 4, k] + (rz * to_primal + sign * (ry * to_dual) + z * to_same)
@@ -336,6 +336,41 @@
     yz_into(ENDS, get, tf, lambda a, k: (a // 4, k), cells, final)
 
 
+def whole_traces(ref):
+    return lambda comp, k: ref[comp, k]
+
+
+def pack_traces(msg, seen, ref, row, side):
+    for k in range(25):
+        ref[k] = jnp.where(row < 4, msg[0, k], swap4(msg[1, k]))
+    for i in range(13):
+        k, later = 2 * i, min(2 * i + 1, 24)
+        ref[25 + i] = rows(
+            row,
+            pltpu.roll(msg[0, k], 2, 0),
+            swap4(msg[1, k]),
+            pltpu.roll(msg[0, later], 6, 0),
+            msg[1, later],
+        )
+    total = Total(jnp.zeros((8, 128), F32))
+    for k in range(25):
+        for comp in range(2):
+            w = LIFT * node_weight(side, k)
+            total.add(pltpu.roll(seen[comp, k], 2, 0) * (msg[comp, k] * w))
+    ref[38] = swap4(total.value())
+
+
+def packed_traces(ref, row):
+    def plane(comp, k):
+        early = ref[k] if comp == 0 else swap4(ref[k])
+        shift = ((6, 2), (4, 0))[comp][k % 2]
+        late = ref[25 + k // 2]
+        late = pltpu.roll(late, shift, 0) if shift else late
+        return jnp.where(row < 4, early, jnp.where(row < 6, 0.0, late))
+
+    return plane
+
+
 def old_plane(sf, si, comp, a, k):
     return sf[comp, a // 4, k] if a in ENDS else si[comp, a - 1, k]
 
@@ -392,7 +427,7 @@
 
 def second_kernel(
     sf_in, si, ci, lo_own, hi_own, below, above, aux, layer, cell, node_ref, amp,
-    s, sf, lo_ref, hi_ref, g_ref, tf,
+    s, sf, lo_ref, hi_ref, g_ref, lo_pack, hi_pack, tf,
 ):
     row, lane = iotas()
     cells = Cells(row, lane)
@@ -408,7 +443,7 @@
             s[comp, 25 * a + k] = new
             total.add(pltpu.roll(inc, 2, 0) * (new * node_weight(a, k)))
 
-    even_half(sf, si, ci, tf, below, above, lo_own, hi_own, row, m_t, cells, final)
+    even_half(sf, si, ci, tf, whole_traces(below), whole_traces(above), lo_own, hi_own, row, m_t, cells, final)
     g = total.value()
     node = node_ref[0]
     w = weight_at(node // 25) * weight_at((node // 5) % 5) * weight_at(node % 5)
@@ -419,6 +454,8 @@
         g = g + pltpu.roll(incs[comp], 2, 0) * (new * w)
     g_ref[...] = g
     odd_ends(s, sf, tf, lo_ref, hi_ref, row, coef, damping, cells)
+    pack_traces(lo_ref, below, lo_pack, row, 0)
+    pack_traces(hi_ref, above, hi_pack, row, 4)
 
 
 def third_kernel(
@@ -438,12 +475,17 @@
             s[comp, 25 * a + k] = (old + inc) * node_weight(a, k)
             total.add(inc[0:2] * cot[comp, 25 * a + k])
 
-    even_half(sf, si, ci, tf, below, above, lo_own, hi_own, row, m_t, cells, final)
+    even_half(
+        sf, si, ci, tf, packed_traces(below, row), packed_traces(above, row), lo_own, hi_own, row, m_t, cells, final
+    )
     g = total.value()
     node = node_ref[0]
     incs = source_planes(1, layer, cell, amp, row, lane, coef)
     for comp in range(3):
         g = g + incs[comp][0:2] * cot[comp, node]
+    position, last = lax.axis_index("space"), lax.axis_size("space") - 1
+    g = g + below[38, 0:2] * (position > 0).astype(F32)
+    g = g + above[38, 0:2] * (position < last).astype(F32)
     g = g + g_in[2:4]
     g_ref[...] = g * coef[0:2] * (-1.0 / DT)
 
@@ -473,6 +515,7 @@
 FACES = (3, 2, 25, 8, 128)
 INNER = (3, 3, 25, 8, 128)
 TRACE = (2, 25, 8, 128)
+PACKED = (39, 8, 128)
 
 
 def exchange(lo, hi):
@@ -531,17 +574,25 @@
     )(f, cot, perm, reg, conductance)
     below, above = exchange(lo, hi)
     si, ci = inner(s, aux)
-    s, sf, lo, hi, g = pl.pallas_call(
+    s, sf, lo, hi, g, lo_pack, hi_pack = pl.pallas_call(
         second_kernel,
-        out_shape=(struct(*STATE), struct(*FACES), struct(*TRACE), struct(*TRACE), struct(8, 128)),
+        out_shape=(
+            struct(*STATE),
+            struct(*FACES),
+            struct(*TRACE),
+            struct(*TRACE),
+            struct(8, 128),
+            struct(*PACKED),
+            struct(*PACKED),
+        ),
         in_specs=[VMEM] * 8 + [SMEM] * 4,
-        out_specs=[VMEM] * 5,
+        out_specs=[VMEM] * 7,
         input_output_aliases={0: 1},
         scratch_shapes=[pltpu.VMEM(FACES, F32)],
         compiler_params=PARAMS,
         name="second",
     )(sf, si, ci, lo, hi, below, above, aux, *source)
-    below, above = exchange(lo, hi)
+    below, above = exchange(lo_pack, hi_pack)
     si, ci = inner(s, aux)
     s, g, _ = pl.pallas_call(
         third_kernel,

time: 51.8 us -> 50.8 us (0.981)
  waiting for transfers between devices: 13.3 us -> 11.3 us
  starting transfers between devices: 24.9 us -> 25.8 us
    ppermute x2, waiting for transfers between devices: 9.81 us -> 7.13 us  [exchange(): got_one = lax.ppermute(one, 'space', outer_pairs)]
    ppermute x6, starting transfers between devices: 6.77 us -> 7.73 us  [src_sum(): lax.ppermute(x, 'src', [(i, i ^ d) for i in range(16)])]
    ppermute x6, waiting for transfers between devices: 3.49 us -> 4.15 us  [src_sum(): lax.ppermute(x, 'src', [(i, i ^ d) for i in range(16)])]
  transfers between devices with their start and end apart: 10 -> 10, of which waited for: 4 -> 5; matrix products, arithmetic and copies ran while one was open for 0% -> 0% of each run, Pallas kernels for 7% -> 7%
where the time goes in v4:
time: 50.8 us; the launch traced here: 50.7 us
  starting transfers between devices  25.8 us (51%)
  waiting for transfers between devices  11.3 us (22%)
  Pallas kernels  10.1 us (20%)
  between operations  2.68 us (5%)
  other arithmetic  0.72 us (1%)
    ppermute x2, starting transfers between devices, exchange(): got_one = lax.ppermute(one, 'space', outer_pairs)  18.1 us
    ppermute x6, starting transfers between devices, src_sum(): lax.ppermute(x, 'src', [(i, i ^ d) for i in range(16)])  7.73 us
    ppermute x2, waiting for transfers between devices, exchange(): got_one = lax.ppermute(one, 'space', outer_pairs)  7.13 us
    ppermute x6, waiting for transfers between devices, src_sum(): lax.ppermute(x, 'src', [(i, i ^ d) for i in range(16)])  4.15 us
    pallas_call x2, Pallas kernels, on_device(): si, ci = inner(s, aux)  2.65 us
    pallas_call x1, Pallas kernels, on_device(): pl.pallas_call(second_kernel, out_shape=(struct(*STATE), struct(*FACES),...  2.61 us
    pallas_call x1, Pallas kernels, on_device(): pl.pallas_call(first_kernel, out_shape=(struct(*STATE), struct(*FACES), s...  2.17 us
    pallas_call x1, Pallas kernels, on_device(): pl.pallas_call(third_kernel, out_shape=(struct(*STATE), struct(2, 128), s...  1.8 us
  transfers between devices with their start and end apart: 10, of which 5 were waited for; matrix products, arithmetic and copies ran while one was open for 0% of the time, Pallas kernels for 7%

profile of v4, /device:TPU:1, one launch (start us, length us, event | category | flops | bytes accessed | tf_op | source)
XLA Modules:
  0.0 50.7 jit_solution(6912805822569228215)
XLA Ops:
  0.6 2.2 %first.1 = (f32[3,125,8,128]{3,2,1,0:T(8,128)S(1)}, f32[3,2,25,8,128]{4,3,2,1,0:T(8,128)S(1)}, f32[2,25,8,128]{3,2,1,0:T(8,128)S(1)}, f32[2,25,8,128]{3,2,1,0:T(8,128)S(1)}, f32[2,8,128]{2,1,0:T(8,128)S(1)}) custom-call(f32[6,125,2,128]{3,2,1,0:T(2,128)} %bitcast.8, f32[6,125,2,128]{3,2,1,0:T(2,128)} %bitcast.6, f32[2,128]{1,0:T(2,128)} %bitcast.11, ...), custom_call_target="tpu_custom_call" | custom-call | tf_op jit(solution)/shard_map/first/pallas_call | solution.py:560
  2.8 0.0 copy-start.1
  2.9 9.4 %collective-permute-start = (f32[2,25,8,128]{3,2,1,0:T(8,128)S(1)}, f32[2,25,8,128]{3,2,1,0:T(8,128)S(1)}, u32[]{:S(2)}, u32[]{:S(2)}) collective-permute-start(f32[2,25,8,128]{3,2,1,0:T(8,128)S(1)} %get-tuple-element.31), channel_id=1, source_target_pairs={{0,240},{16,32},{32,16},{48,64},{64,48},{80,96},{96,80},{112,128},... | collective-permute-start | bytes 614408 | tf_op jit(solution)/shard_map/ppermute | solution.py:527
  12.3 0.0 collective-permute-start.1
  14.2 1.3 %inner.2 = (f32[3,3,25,8,128]{4,3,2,1,0:T(8,128)S(1)}, f32[3,125,8,128]{3,2,1,0:T(8,128)S(1)}) custom-call(f32[3,125,8,128]{3,2,1,0:T(8,128)S(1)} %get-tuple-element.25.s, f32[2,8,128]{2,1,0:T(8,128)S(1)} %get-tuple-element.26.aux), custom_call_target="tpu_custom_call" | custom-call | flops 20000000 | bytes 1000 | tf_op jit(solution)/shard_map/inner/pallas_call | solution.py:576
  15.5 2.7 %collective-permute-done = f32[2,25,8,128]{3,2,1,0:T(8,128)S(1)} collective-permute-done((f32[2,25,8,128]{3,2,1,0:T(8,128)S(1)}, f32[2,25,8,128]{3,2,1,0:T(8,128)S(1)}, u32[]{:S(2)}, u32[]{:S(2)}) %collective-permute-start) | collective-permute-done | bytes 204832 | tf_op jit(solution)/shard_map/ppermute | solution.py:527
  18.2 0.0 collective-permute-done.1
  18.3 0.0 copy-done.1
  18.3 2.6 %second.1 = (f32[3,125,8,128]{3,2,1,0:T(8,128)S(1)}, f32[3,2,25,8,128]{4,3,2,1,0:T(8,128)S(1)}, f32[2,25,8,128]{3,2,1,0:T(8,128)S(1)}, f32[2,25,8,128]{3,2,1,0:T...) custom-call(f32[3,2,25,8,128]{4,3,2,1,0:T(8,128)S(1)} %get-tuple-ele, ...), custom_call_target="tpu_custom_call", output_to_operand_aliasing={{1}: (0, {})} | custom-call | tf_op jit(solution)/shard_map/second/pallas_call | solution.py:577
  20.9 0.0 copy-start
  21.0 8.7 %collective-permute-start.2 = (f32[39,8,128]{2,1,0:T(8,128)S(1)}, f32[39,8,128]{2,1,0:T(8,128)S(1)}, u32[]{:S(2)}, u32[]{:S(2)}) collective-permute-start(f32[39,8,128]{2,1,0:T(8,128)S(1)} %get-tuple-element.41), channel_id=1, source_target_pairs={{0,240},{16,32},{32,16},{48,64},{64,48},{80,96},{96,80},{112,128},... | collective-permute-start | bytes 479240 | tf_op jit(solution)/shard_map/ppermute | solution.py:527
  29.7 0.0 collective-permute-start.3
  29.7 1.3 %inner.3 = (f32[3,3,25,8,128]{4,3,2,1,0:T(8,128)S(1)}, f32[3,125,8,128]{3,2,1,0:T(8,128)S(1)}) custom-call(f32[3,125,8,128]{3,2,1,0:T(8,128)S(1)} %get-tuple-element.34.s, f32[2,8,128]{2,1,0:T(8,128)S(1)} %get-tuple-element.26.aux), custom_call_target="tpu_custom_call" | custom-call | flops 20000000 | bytes 1000 | tf_op jit(solution)/shard_map/inner/pallas_call | solution.py:596
  31.0 4.4 %collective-permute-done.2 = f32[39,8,128]{2,1,0:T(8,128)S(1)} collective-permute-done((f32[39,8,128]{2,1,0:T(8,128)S(1)}, f32[39,8,128]{2,1,0:T(8,128)S(1)}, u32[]{:S(2)}, u32[]{:S(2)}) %collective-permute-start.2) | collective-permute-done | bytes 159776 | tf_op jit(solution)/shard_map/ppermute | solution.py:527
  35.4 0.0 collective-permute-done.3
  35.5 0.0 copy-done
  35.5 1.8 %third.1 = (f32[3,125,8,128]{3,2,1,0:T(8,128)S(1)}, f32[2,128]{1,0:T(2,128)S(1)}, f32[3,2,25,8,128]{4,3,2,1,0:T(8,128)S(1)}) custom-call(f32[3,2,25,8,128]{4,3,2,1,0:T(8,128)S(1)} %get-tuple-element.33.sf_in, f32[3,3,25,8,128]{4,3,2,1,0:T(8,128)S(1)} %get-tuple-element.35.si, ...), custom_call_target="tpu_custom_call", output_to_operand_aliasing={{2}: (0, {})} | custom-call | tf_op jit(solution)/shard_map/third/pallas_call | solution.py:597
  37.3 3.9 %collective-permute-start.6 = (f32[2,128]{1,0:T(2,128)S(1)}, f32[2,128]{1,0:T(2,128)S(1)}, u32[]{:S(2)}, u32[]{:S(2)}) collective-permute-start(f32[2,128]{1,0:T(2,128)S(1)} %get-tuple-element.45), channel_id=1, source_target_pairs={{0,3},{1,2},{2,1},{3,0},{4,7},{5,6},{6,5},{7,4},{8,11},{9,10},{10,... | collective-permute-start | bytes 3080 | tf_op jit(solution)/shard_map/ppermute | solution.py:534
  41.2 0.1 collective-permute-start.5
  41.3 0.4 collective-permute-start.4
  41.7 0.8 %collective-permute-done.6 = f32[2,128]{1,0:T(2,128)S(1)} collective-permute-done((f32[2,128]{1,0:T(2,128)S(1)}, f32[2,128]{1,0:T(2,128)S(1)}, u32[]{:S(2)}, u32[]{:S(2)}) %collective-permute-start.6) | collective-permute-done | bytes 1056 | tf_op jit(solution)/shard_map/ppermute | solution.py:534
  42.5 1.1 %collective-permute-done.5 = f32[2,128]{1,0:T(2,128)S(1)} collective-permute-done((f32[2,128]{1,0:T(2,128)S(1)}, f32[2,128]{1,0:T(2,128)S(1)}, u32[]{:S(2)}, u32[]{:S(2)}) %collective-permute-start.5) | collective-permute-done | bytes 1056 | tf_op jit(solution)/shard_map/ppermute | solution.py:534
  43.6 0.0 collective-permute-done.4
  43.6 2.6 %collective-permute-start.9 = (f32[2,128]{1,0:T(2,128)S(1)}, f32[2,128]{1,0:T(2,128)S(1)}, u32[]{:S(2)}, u32[]{:S(2)}) collective-permute-start(f32[2,128]{1,0:T(2,128)S(1)} %add_add_fusion.1), channel_id=1, source_target_pairs={{0,12},{1,13},{2,14},{3,15},{4,8},{5,9},{6,10},{7,11},{8,4},{9,5},... | collective-permute-start | bytes 3080 | tf_op jit(solution)/shard_map/ppermute | solution.py:534
  46.2 0.5 %collective-permute-start.8 = (f32[2,128]{1,0:T(2,128)S(1)}, f32[2,128]{1,0:T(2,128)S(1)}, u32[]{:S(2)}, u32[]{:S(2)}) collective-permute-start(f32[2,128]{1,0:T(2,128)S(1)} %add_add_fusion.1), channel_id=1, source_target_pairs={{0,8},{1,9},{2,10},{3,11},{4,12},{5,13},{6,14},{7,15},{8,0},{9,1},... | collective-permute-start | bytes 3080 | tf_op jit(solution)/shard_map/ppermute | solution.py:534
  46.7 0.3 collective-permute-start.7
  46.9 0.9 %store.1 = f32[6,125,2,128]{3,2,1,0:T(2,128)} custom-call(f32[3,125,8,128]{3,2,1,0:T(8,128)S(1)} %get-tuple-element.44.s), custom_call_target="tpu_custom_call" | custom-call | bytes 4000000 | tf_op jit(solution)/shard_map/store/pallas_call | solution.py:607
  47.8 0.0 collective-permute-done.9
  47.8 2.2 %collective-permute-done.8 = f32[2,128]{1,0:T(2,128)S(1)} collective-permute-done((f32[2,128]{1,0:T(2,128)S(1)}, f32[2,128]{1,0:T(2,128)S(1)}, u32[]{:S(2)}, u32[]{:S(2)}) %collective-permute-start.8) | collective-permute-done | bytes 1056 | tf_op jit(solution)/shard_map/ppermute | solution.py:534
  50.1 0.0 collective-permute-done.7
  50.1 0.6 %add_add_fusion = f32[2,128]{1,0:T(2,128)} fusion(f32[2,128]{1,0:T(2,128)S(1)} %collective-permute-done.8, f32[2,128]{1,0:T(2,128)S(1)} %collective-permute-done.9, f32[2,128]{1,0:T(2,128)S(1)} %add_add_fusion.1, f32[2,128]{1,0:T(2,128)S(1)} %collective-permute-done.7), kind=kLoop, calls=%fused_computation.8 | loop fusion | flops 768 | bytes 5120 | tf_op jit(solution)/shard_map/add | solution.py:535
  (5 shorter events, 0.1 us)
Async XLA Ops:
  2.8 15.5 %copy-start.1 = (f32[1,6]{1,0:T(1,128)S(1)}, f32[1,6]{1,0:T(1,128)}, u32[]{:S(2)}) copy-start(f32[1,6]{1,0:T(1,128)} %amp.3) | copy-start | bytes 76
  2.9 15.4 %collective-permute-start = (f32[2,25,8,128]{3,2,1,0:T(8,128)S(1)}, f32[2,25,8,128]{3,2,1,0:T(8,128)S(1)}, u32[]{:S(2)}, u32[]{:S(2)}) collective-permute-start(f32[2,25,8,128]{3,2,1,0:T(8,128)S(1)} %get-tuple-element.31), channel_id=1, source_target_pairs={{0,240},{16,32},{32,16},{48,64},{64,48},{80,96},{96,80},{112,128},... | collective-permute-start | bytes 614408 | tf_op jit(solution)/shard_map/ppermute | solution.py:527
  12.3 6.0 %collective-permute-start.1 = (f32[2,25,8,128]{3,2,1,0:T(8,128)S(1)}, f32[2,25,8,128]{3,2,1,0:T(8,128)S(1)}, u32[]{:S(2)}, u32[]{:S(2)}) collective-permute-start(f32[2,25,8,128]{3,2,1,0:T(8,128)S(1)} %get-tuple-element.32), channel_id=1, source_target_pairs={{0,16},{16,0},{32,48},{48,32},{64,80},{80,64},{96,112},{112,96},{1... | collective-permute-start | bytes 614408 | tf_op jit(solution)/shard_map/ppermute | solution.py:528
  20.9 14.6 %copy-start = (f32[6,125,1,1,256]{4,3,2,1,0:T(1,128)S(1)}, f32[6,125,1,1,256]{4,3,2,1,0:T(1,128)}, u32[]{:S(2)}) copy-start(f32[6,125,1,1,256]{4,3,2,1,0:T(1,128)} %param.10) | copy-start | bytes 2304004
  21.0 14.5 %collective-permute-start.2 = (f32[39,8,128]{2,1,0:T(8,128)S(1)}, f32[39,8,128]{2,1,0:T(8,128)S(1)}, u32[]{:S(2)}, u32[]{:S(2)}) collective-permute-start(f32[39,8,128]{2,1,0:T(8,128)S(1)} %get-tuple-element.41), channel_id=1, source_target_pairs={{0,240},{16,32},{32,16},{48,64},{64,48},{80,96},{96,80},{112,128},... | collective-permute-start | bytes 479240 | tf_op jit(solution)/shard_map/ppermute | solution.py:527
  29.7 5.8 %collective-permute-start.3 = (f32[39,8,128]{2,1,0:T(8,128)S(1)}, f32[39,8,128]{2,1,0:T(8,128)S(1)}, u32[]{:S(2)}, u32[]{:S(2)}) collective-permute-start(f32[39,8,128]{2,1,0:T(8,128)S(1)} %get-tuple-element.42), channel_id=1, source_target_pairs={{0,16},{16,0},{32,48},{48,32},{64,80},{80,64},{96,112},{112,96},{1... | collective-permute-start | bytes 479240 | tf_op jit(solution)/shard_map/ppermute | solution.py:528
  37.3 5.2 %collective-permute-start.6 = (f32[2,128]{1,0:T(2,128)S(1)}, f32[2,128]{1,0:T(2,128)S(1)}, u32[]{:S(2)}, u32[]{:S(2)}) collective-permute-start(f32[2,128]{1,0:T(2,128)S(1)} %get-tuple-element.45), channel_id=1, source_target_pairs={{0,3},{1,2},{2,1},{3,0},{4,7},{5,6},{6,5},{7,4},{8,11},{9,10},{10,... | collective-permute-start | bytes 3080 | tf_op jit(solution)/shard_map/ppermute | solution.py:534
  41.2 2.4 %collective-permute-start.5 = (f32[2,128]{1,0:T(2,128)S(1)}, f32[2,128]{1,0:T(2,128)S(1)}, u32[]{:S(2)}, u32[]{:S(2)}) collective-permute-start(f32[2,128]{1,0:T(2,128)S(1)} %get-tuple-element.45), channel_id=1, source_target_pairs={{0,2},{1,3},{2,0},{3,1},{4,6},{5,7},{6,4},{7,5},{8,10},{9,11},{10,... | collective-permute-start | bytes 3080 | tf_op jit(solution)/shard_map/ppermute | solution.py:534
  41.3 2.3 %collective-permute-start.4 = (f32[2,128]{1,0:T(2,128)S(1)}, f32[2,128]{1,0:T(2,128)S(1)}, u32[]{:S(2)}, u32[]{:S(2)}) collective-permute-start(f32[2,128]{1,0:T(2,128)S(1)} %get-tuple-element.45), channel_id=1, source_target_pairs={{0,1},{1,0},{2,3},{3,2},{4,5},{5,4},{6,7},{7,6},{8,9},{9,8},{10,11... | collective-permute-start | bytes 3080 | tf_op jit(solution)/shard_map/ppermute | solution.py:534
  43.6 4.2 %collective-permute-start.9 = (f32[2,128]{1,0:T(2,128)S(1)}, f32[2,128]{1,0:T(2,128)S(1)}, u32[]{:S(2)}, u32[]{:S(2)}) collective-permute-start(f32[2,128]{1,0:T(2,128)S(1)} %add_add_fusion.1), channel_id=1, source_target_pairs={{0,12},{1,13},{2,14},{3,15},{4,8},{5,9},{6,10},{7,11},{8,4},{9,5},... | collective-permute-start | bytes 3080 | tf_op jit(solution)/shard_map/ppermute | solution.py:534
  46.2 3.9 %collective-permute-start.8 = (f32[2,128]{1,0:T(2,128)S(1)}, f32[2,128]{1,0:T(2,128)S(1)}, u32[]{:S(2)}, u32[]{:S(2)}) collective-permute-start(f32[2,128]{1,0:T(2,128)S(1)} %add_add_fusion.1), channel_id=1, source_target_pairs={{0,8},{1,9},{2,10},{3,11},{4,12},{5,13},{6,14},{7,15},{8,0},{9,1},... | collective-permute-start | bytes 3080 | tf_op jit(solution)/shard_map/ppermute | solution.py:534
  46.7 3.4 %collective-permute-start.7 = (f32[2,128]{1,0:T(2,128)S(1)}, f32[2,128]{1,0:T(2,128)S(1)}, u32[]{:S(2)}, u32[]{:S(2)}) collective-permute-start(f32[2,128]{1,0:T(2,128)S(1)} %add_add_fusion.1), channel_id=1, source_target_pairs={{0,4},{1,5},{2,6},{3,7},{4,0},{5,1},{6,2},{7,3},{8,12},{9,13},{10,... | collective-permute-start | bytes 3080 | tf_op jit(solution)/shard_map/ppermute | solution.py:534

commit v5 on v4

--- a/solution.py
+++ b/solution.py
@@ -522,7 +522,7 @@
     peers = lax.axis_size("space")
     even = lax.axis_index("space") % 2 == 0
     inner_pairs = [(i, i ^ 1) for i in range(peers)]
-    outer_pairs = [(i, (i + 2 * (i % 2) - 1) % peers) for i in range(peers)]
+    outer_pairs = [(i, i + 2 * (i % 2) - 1) for i in range(1, peers - 1)]
     one, two = lax.optimization_barrier((jnp.where(even, lo, hi), jnp.where(even, hi, lo)))
     got_one = lax.ppermute(one, "space", outer_pairs)
     got_two = lax.ppermute(two, "space", inner_pairs)

time: 50.8 us -> 50.5 us (level)
  the two profiles are of different devices: /device:TPU:1 before, /device:TPU:160 now
where the time goes in v5:
time: 50.5 us; the launch traced here: 50.3 us
  waiting for transfers between devices  22.3 us (44%)
  starting transfers between devices  14.5 us (29%)
  Pallas kernels  10.1 us (20%)
  between operations  2.71 us (5%)
  other arithmetic  0.72 us (1%)
    ppermute x2, waiting for transfers between devices, exchange(): got_one = lax.ppermute(one, 'space', outer_pairs)  17.6 us
    ppermute x2, starting transfers between devices, exchange(): got_one = lax.ppermute(one, 'space', outer_pairs)  8.03 us
    ppermute x6, starting transfers between devices, src_sum(): lax.ppermute(x, 'src', [(i, i ^ d) for i in range(16)])  6.12 us
    ppermute x6, waiting for transfers between devices, src_sum(): lax.ppermute(x, 'src', [(i, i ^ d) for i in range(16)])  4.65 us
    pallas_call x2, Pallas kernels, on_device(): si, ci = inner(s, aux)  2.66 us
    pallas_call x1, Pallas kernels, on_device(): pl.pallas_call(second_kernel, out_shape=(struct(*STATE), struct(*FACES),...  2.61 us
    pallas_call x1, Pallas kernels, on_device(): pl.pallas_call(first_kernel, out_shape=(struct(*STATE), struct(*FACES), s...  2.17 us
    pallas_call x1, Pallas kernels, on_device(): pl.pallas_call(third_kernel, out_shape=(struct(*STATE), struct(2, 128), s...  1.8 us
  transfers between devices with their start and end apart: 10, of which 5 were waited for; matrix products, arithmetic and copies ran while one was open for 0% of the time, Pallas kernels for 7%

profile of v5, /device:TPU:160, one launch (start us, length us, event | category | flops | bytes accessed | tf_op | source)
XLA Modules:
  0.0 50.3 jit_solution(6613448396490520620)
XLA Ops:
  0.6 2.2 %first.1 = (f32[3,125,8,128]{3,2,1,0:T(8,128)S(1)}, f32[3,2,25,8,128]{4,3,2,1,0:T(8,128)S(1)}, f32[2,25,8,128]{3,2,1,0:T(8,128)S(1)}, f32[2,25,8,128]{3,2,1,0:T(8,128)S(1)}, f32[2,8,128]{2,1,0:T(8,128)S(1)}) custom-call(f32[6,125,2,128]{3,2,1,0:T(2,128)} %bitcast.8, f32[6,125,2,128]{3,2,1,0:T(2,128)} %bitcast.6, f32[2,128]{1,0:T(2,128)} %bitcast.11, ...), custom_call_target="tpu_custom_call" | custom-call | tf_op jit(solution)/shard_map/first/pallas_call | solution.py:560
  2.8 0.0 copy-start.1
  2.9 4.9 %collective-permute-start = (f32[2,25,8,128]{3,2,1,0:T(8,128)S(1)}, f32[2,25,8,128]{3,2,1,0:T(8,128)S(1)}, u32[]{:S(2)}, u32[]{:S(2)}) collective-permute-start(f32[2,25,8,128]{3,2,1,0:T(8,128)S(1)} %get-tuple-element.31), channel_id=1, source_target_pairs={{16,32},{32,16},{48,64},{64,48},{80,96},{96,80},{112,128},{128,112... | collective-permute-start | bytes 614408 | tf_op jit(solution)/shard_map/ppermute | solution.py:527
  7.8 0.2 collective-permute-start.1
  10.0 1.3 %inner.2 = (f32[3,3,25,8,128]{4,3,2,1,0:T(8,128)S(1)}, f32[3,125,8,128]{3,2,1,0:T(8,128)S(1)}) custom-call(f32[3,125,8,128]{3,2,1,0:T(8,128)S(1)} %get-tuple-element.25.s, f32[2,8,128]{2,1,0:T(8,128)S(1)} %get-tuple-element.26.aux), custom_call_target="tpu_custom_call" | custom-call | flops 20000000 | bytes 1000 | tf_op jit(solution)/shard_map/inner/pallas_call | solution.py:576
  11.3 7.0 %collective-permute-done = f32[2,25,8,128]{3,2,1,0:T(8,128)S(1)} collective-permute-done((f32[2,25,8,128]{3,2,1,0:T(8,128)S(1)}, f32[2,25,8,128]{3,2,1,0:T(8,128)S(1)}, u32[]{:S(2)}, u32[]{:S(2)}) %collective-permute-start) | collective-permute-done | bytes 204832 | tf_op jit(solution)/shard_map/ppermute | solution.py:527
  18.3 0.0 collective-permute-done.1
  18.4 0.0 copy-done.1
  18.4 2.6 %second.1 = (f32[3,125,8,128]{3,2,1,0:T(8,128)S(1)}, f32[3,2,25,8,128]{4,3,2,1,0:T(8,128)S(1)}, f32[2,25,8,128]{3,2,1,0:T(8,128)S(1)}, f32[2,25,8,128]{3,2,1,0:T...) custom-call(f32[3,2,25,8,128]{4,3,2,1,0:T(8,128)S(1)} %get-tuple-ele, ...), custom_call_target="tpu_custom_call", output_to_operand_aliasing={{1}: (0, {})} | custom-call | tf_op jit(solution)/shard_map/second/pallas_call | solution.py:577
  21.0 0.0 copy-start
  21.0 3.1 %collective-permute-start.2 = (f32[39,8,128]{2,1,0:T(8,128)S(1)}, f32[39,8,128]{2,1,0:T(8,128)S(1)}, u32[]{:S(2)}, u32[]{:S(2)}) collective-permute-start(f32[39,8,128]{2,1,0:T(8,128)S(1)} %get-tuple-element.41), channel_id=1, source_target_pairs={{16,32},{32,16},{48,64},{64,48},{80,96},{96,80},{112,128},{128,112... | collective-permute-start | bytes 479240 | tf_op jit(solution)/shard_map/ppermute | solution.py:527
  24.2 0.1 collective-permute-start.3
  24.3 1.3 %inner.3 = (f32[3,3,25,8,128]{4,3,2,1,0:T(8,128)S(1)}, f32[3,125,8,128]{3,2,1,0:T(8,128)S(1)}) custom-call(f32[3,125,8,128]{3,2,1,0:T(8,128)S(1)} %get-tuple-element.34.s, f32[2,8,128]{2,1,0:T(8,128)S(1)} %get-tuple-element.26.aux), custom_call_target="tpu_custom_call" | custom-call | flops 20000000 | bytes 1000 | tf_op jit(solution)/shard_map/inner/pallas_call | solution.py:596
  25.6 10.6 %collective-permute-done.2 = f32[39,8,128]{2,1,0:T(8,128)S(1)} collective-permute-done((f32[39,8,128]{2,1,0:T(8,128)S(1)}, f32[39,8,128]{2,1,0:T(8,128)S(1)}, u32[]{:S(2)}, u32[]{:S(2)}) %collective-permute-start.2) | collective-permute-done | bytes 159776 | tf_op jit(solution)/shard_map/ppermute | solution.py:527
  36.2 0.0 collective-permute-done.3
  36.3 0.0 copy-done
  36.3 1.8 %third.1 = (f32[3,125,8,128]{3,2,1,0:T(8,128)S(1)}, f32[2,128]{1,0:T(2,128)S(1)}, f32[3,2,25,8,128]{4,3,2,1,0:T(8,128)S(1)}) custom-call(f32[3,2,25,8,128]{4,3,2,1,0:T(8,128)S(1)} %get-tuple-element.33.sf_in, f32[3,3,25,8,128]{4,3,2,1,0:T(8,128)S(1)} %get-tuple-element.35.si, ...), custom_call_target="tpu_custom_call", output_to_operand_aliasing={{2}: (0, {})} | custom-call | tf_op jit(solution)/shard_map/third/pallas_call | solution.py:597
  38.1 0.1 collective-permute-start.6
  38.2 0.3 collective-permute-start.5
  38.5 1.6 %collective-permute-start.4 = (f32[2,128]{1,0:T(2,128)S(1)}, f32[2,128]{1,0:T(2,128)S(1)}, u32[]{:S(2)}, u32[]{:S(2)}) collective-permute-start(f32[2,128]{1,0:T(2,128)S(1)} %get-tuple-element.45), channel_id=1, source_target_pairs={{0,1},{1,0},{2,3},{3,2},{4,5},{5,4},{6,7},{7,6},{8,9},{9,8},{10,11... | collective-permute-start | bytes 3080 | tf_op jit(solution)/shard_map/ppermute | solution.py:534
  40.0 1.1 %collective-permute-done.6 = f32[2,128]{1,0:T(2,128)S(1)} collective-permute-done((f32[2,128]{1,0:T(2,128)S(1)}, f32[2,128]{1,0:T(2,128)S(1)}, u32[]{:S(2)}, u32[]{:S(2)}) %collective-permute-start.6) | collective-permute-done | bytes 1056 | tf_op jit(solution)/shard_map/ppermute | solution.py:534
  41.2 0.7 %collective-permute-done.5 = f32[2,128]{1,0:T(2,128)S(1)} collective-permute-done((f32[2,128]{1,0:T(2,128)S(1)}, f32[2,128]{1,0:T(2,128)S(1)}, u32[]{:S(2)}, u32[]{:S(2)}) %collective-permute-start.5) | collective-permute-done | bytes 1056 | tf_op jit(solution)/shard_map/ppermute | solution.py:534
  41.8 0.0 collective-permute-done.4
  41.8 2.8 %collective-permute-start.9 = (f32[2,128]{1,0:T(2,128)S(1)}, f32[2,128]{1,0:T(2,128)S(1)}, u32[]{:S(2)}, u32[]{:S(2)}) collective-permute-start(f32[2,128]{1,0:T(2,128)S(1)} %add_add_fusion.1), channel_id=1, source_target_pairs={{0,12},{1,13},{2,14},{3,15},{4,8},{5,9},{6,10},{7,11},{8,4},{9,5},... | collective-permute-start | bytes 3080 | tf_op jit(solution)/shard_map/ppermute | solution.py:534
  44.7 0.8 %collective-permute-start.8 = (f32[2,128]{1,0:T(2,128)S(1)}, f32[2,128]{1,0:T(2,128)S(1)}, u32[]{:S(2)}, u32[]{:S(2)}) collective-permute-start(f32[2,128]{1,0:T(2,128)S(1)} %add_add_fusion.1), channel_id=1, source_target_pairs={{0,8},{1,9},{2,10},{3,11},{4,12},{5,13},{6,14},{7,15},{8,0},{9,1},... | collective-permute-start | bytes 3080 | tf_op jit(solution)/shard_map/ppermute | solution.py:534
  45.5 0.5 %collective-permute-start.7 = (f32[2,128]{1,0:T(2,128)S(1)}, f32[2,128]{1,0:T(2,128)S(1)}, u32[]{:S(2)}, u32[]{:S(2)}) collective-permute-start(f32[2,128]{1,0:T(2,128)S(1)} %add_add_fusion.1), channel_id=1, source_target_pairs={{0,4},{1,5},{2,6},{3,7},{4,0},{5,1},{6,2},{7,3},{8,12},{9,13},{10,... | collective-permute-start | bytes 3080 | tf_op jit(solution)/shard_map/ppermute | solution.py:534
  46.0 0.9 %store.1 = f32[6,125,2,128]{3,2,1,0:T(2,128)} custom-call(f32[3,125,8,128]{3,2,1,0:T(8,128)S(1)} %get-tuple-element.44.s), custom_call_target="tpu_custom_call" | custom-call | bytes 4000000 | tf_op jit(solution)/shard_map/store/pallas_call | solution.py:607
  46.9 0.0 collective-permute-done.9
  46.9 2.8 %collective-permute-done.8 = f32[2,128]{1,0:T(2,128)S(1)} collective-permute-done((f32[2,128]{1,0:T(2,128)S(1)}, f32[2,128]{1,0:T(2,128)S(1)}, u32[]{:S(2)}, u32[]{:S(2)}) %collective-permute-start.8) | collective-permute-done | bytes 1056 | tf_op jit(solution)/shard_map/ppermute | solution.py:534
  49.8 0.0 collective-permute-done.7
  49.8 0.6 %add_add_fusion = f32[2,128]{1,0:T(2,128)} fusion(f32[2,128]{1,0:T(2,128)S(1)} %collective-permute-done.8, f32[2,128]{1,0:T(2,128)S(1)} %collective-permute-done.9, f32[2,128]{1,0:T(2,128)S(1)} %add_add_fusion.1, f32[2,128]{1,0:T(2,128)S(1)} %collective-permute-done.7), kind=kLoop, calls=%fused_computation.8 | loop fusion | flops 768 | bytes 5120 | tf_op jit(solution)/shard_map/add | solution.py:535
  (5 shorter events, 0.1 us)
Async XLA Ops:
  2.8 15.5 %copy-start.1 = (f32[1,6]{1,0:T(1,128)S(1)}, f32[1,6]{1,0:T(1,128)}, u32[]{:S(2)}) copy-start(f32[1,6]{1,0:T(1,128)} %amp.3) | copy-start | bytes 76
  2.9 15.5 %collective-permute-start = (f32[2,25,8,128]{3,2,1,0:T(8,128)S(1)}, f32[2,25,8,128]{3,2,1,0:T(8,128)S(1)}, u32[]{:S(2)}, u32[]{:S(2)}) collective-permute-start(f32[2,25,8,128]{3,2,1,0:T(8,128)S(1)} %get-tuple-element.31), channel_id=1, source_target_pairs={{16,32},{32,16},{48,64},{64,48},{80,96},{96,80},{112,128},{128,112... | collective-permute-start | bytes 614408 | tf_op jit(solution)/shard_map/ppermute | solution.py:527
  7.8 10.5 %collective-permute-start.1 = (f32[2,25,8,128]{3,2,1,0:T(8,128)S(1)}, f32[2,25,8,128]{3,2,1,0:T(8,128)S(1)}, u32[]{:S(2)}, u32[]{:S(2)}) collective-permute-start(f32[2,25,8,128]{3,2,1,0:T(8,128)S(1)} %get-tuple-element.32), channel_id=1, source_target_pairs={{0,16},{16,0},{32,48},{48,32},{64,80},{80,64},{96,112},{112,96},{1... | collective-permute-start | bytes 614408 | tf_op jit(solution)/shard_map/ppermute | solution.py:528
  21.0 15.3 %copy-start = (f32[6,125,1,1,256]{4,3,2,1,0:T(1,128)S(1)}, f32[6,125,1,1,256]{4,3,2,1,0:T(1,128)}, u32[]{:S(2)}) copy-start(f32[6,125,1,1,256]{4,3,2,1,0:T(1,128)} %param.10) | copy-start | bytes 2304004
  21.0 15.2 %collective-permute-start.2 = (f32[39,8,128]{2,1,0:T(8,128)S(1)}, f32[39,8,128]{2,1,0:T(8,128)S(1)}, u32[]{:S(2)}, u32[]{:S(2)}) collective-permute-start(f32[39,8,128]{2,1,0:T(8,128)S(1)} %get-tuple-element.41), channel_id=1, source_target_pairs={{16,32},{32,16},{48,64},{64,48},{80,96},{96,80},{112,128},{128,112... | collective-permute-start | bytes 479240 | tf_op jit(solution)/shard_map/ppermute | solution.py:527
  24.2 12.1 %collective-permute-start.3 = (f32[39,8,128]{2,1,0:T(8,128)S(1)}, f32[39,8,128]{2,1,0:T(8,128)S(1)}, u32[]{:S(2)}, u32[]{:S(2)}) collective-permute-start(f32[39,8,128]{2,1,0:T(8,128)S(1)} %get-tuple-element.42), channel_id=1, source_target_pairs={{0,16},{16,0},{32,48},{48,32},{64,80},{80,64},{96,112},{112,96},{1... | collective-permute-start | bytes 479240 | tf_op jit(solution)/shard_map/ppermute | solution.py:528
  38.1 3.1 %collective-permute-start.6 = (f32[2,128]{1,0:T(2,128)S(1)}, f32[2,128]{1,0:T(2,128)S(1)}, u32[]{:S(2)}, u32[]{:S(2)}) collective-permute-start(f32[2,128]{1,0:T(2,128)S(1)} %get-tuple-element.45), channel_id=1, source_target_pairs={{0,3},{1,2},{2,1},{3,0},{4,7},{5,6},{6,5},{7,4},{8,11},{9,10},{10,... | collective-permute-start | bytes 3080 | tf_op jit(solution)/shard_map/ppermute | solution.py:534
  38.2 3.7 %collective-permute-start.5 = (f32[2,128]{1,0:T(2,128)S(1)}, f32[2,128]{1,0:T(2,128)S(1)}, u32[]{:S(2)}, u32[]{:S(2)}) collective-permute-start(f32[2,128]{1,0:T(2,128)S(1)} %get-tuple-element.45), channel_id=1, source_target_pairs={{0,2},{1,3},{2,0},{3,1},{4,6},{5,7},{6,4},{7,5},{8,10},{9,11},{10,... | collective-permute-start | bytes 3080 | tf_op jit(solution)/shard_map/ppermute | solution.py:534
  38.5 3.4 %collective-permute-start.4 = (f32[2,128]{1,0:T(2,128)S(1)}, f32[2,128]{1,0:T(2,128)S(1)}, u32[]{:S(2)}, u32[]{:S(2)}) collective-permute-start(f32[2,128]{1,0:T(2,128)S(1)} %get-tuple-element.45), channel_id=1, source_target_pairs={{0,1},{1,0},{2,3},{3,2},{4,5},{5,4},{6,7},{7,6},{8,9},{9,8},{10,11... | collective-permute-start | bytes 3080 | tf_op jit(solution)/shard_map/ppermute | solution.py:534
  41.8 5.1 %collective-permute-start.9 = (f32[2,128]{1,0:T(2,128)S(1)}, f32[2,128]{1,0:T(2,128)S(1)}, u32[]{:S(2)}, u32[]{:S(2)}) collective-permute-start(f32[2,128]{1,0:T(2,128)S(1)} %add_add_fusion.1), channel_id=1, source_target_pairs={{0,12},{1,13},{2,14},{3,15},{4,8},{5,9},{6,10},{7,11},{8,4},{9,5},... | collective-permute-start | bytes 3080 | tf_op jit(solution)/shard_map/ppermute | solution.py:534
  44.7 5.1 %collective-permute-start.8 = (f32[2,128]{1,0:T(2,128)S(1)}, f32[2,128]{1,0:T(2,128)S(1)}, u32[]{:S(2)}, u32[]{:S(2)}) collective-permute-start(f32[2,128]{1,0:T(2,128)S(1)} %add_add_fusion.1), channel_id=1, source_target_pairs={{0,8},{1,9},{2,10},{3,11},{4,12},{5,13},{6,14},{7,15},{8,0},{9,1},... | collective-permute-start | bytes 3080 | tf_op jit(solution)/shard_map/ppermute | solution.py:534
  45.5 4.3 %collective-permute-start.7 = (f32[2,128]{1,0:T(2,128)S(1)}, f32[2,128]{1,0:T(2,128)S(1)}, u32[]{:S(2)}, u32[]{:S(2)}) collective-permute-start(f32[2,128]{1,0:T(2,128)S(1)} %add_add_fusion.1), channel_id=1, source_target_pairs={{0,4},{1,5},{2,6},{3,7},{4,0},{5,1},{6,2},{7,3},{8,12},{9,13},{10,... | collective-permute-start | bytes 3080 | tf_op jit(solution)/shard_map/ppermute | solution.py:534
